TPU v7x, 128 devices: a whole 4x4x4 slice. The times are simulated.
128 devices in a mesh: vocab: 4 (over x_hi, core), dp: 32 (over x_lo, z, y).
Axes of the slice: x: 4 (x_hi: 2, x_lo: 2; x = x_hi * 2 + x_lo), y: 4, z: 4, core: 2. Of those that a mesh axis runs over, the one named last changes fastest.
Arguments:
- hidden: bfloat16 [4096, 7168], P('dp'), may hold values from -6 to 6
- gain: float32 [7168], replicated, may hold values from 0.25 to 1.75
- head_weight: bfloat16 [10240, 7168], P(('vocab', 'dp'))
- first_moment: float32 [10240, 7168], P(('vocab', 'dp')), may hold values from -0.12 to 0.12
- second_moment: float32 [10240, 7168], P(('vocab', 'dp')), may hold values from 0.0001 to 0.01
- targets: int32 [4096], P('dp'), may hold values from 0 to 10239
Outputs:
- grad_hidden: bfloat16 [4096, 7168], P('dp')
- grad_gain: float32 [7168], replicated
- new_weight: bfloat16 [10240, 7168], P(('vocab', 'dp'))
- new_first: float32 [10240, 7168], P(('vocab', 'dp'))
- new_second: float32 [10240, 7168], P(('vocab', 'dp'))
All inputs are finite; a program needn't handle non-finite values.
Results may differ from a plain program's by a relative error of at most 0.007.
The roundings to bfloat16 on the way count: a program that leaves them out, or rounds other values in their place, can miss the bound.
Values may be sent and summed in bfloat16 or wider, within the bound.
No kernel may reach another device: no remote copies, remote signals or barrier semaphores. Data moves between devices by JAX's collectives and lax.ppermute only.
A program may use at most 192 MiB of HBM per device.

v0:
```python
import jax
import jax.numpy as jnp
from jax import lax
from jax.sharding import PartitionSpec as P

STEP = 100


def adam_step(weight, first, second, grads):
    new_first = 0.9 * first + 0.1 * grads
    new_second = 0.95 * second + 0.05 * grads * grads
    corr_one = 1.0 - 0.9**STEP
    corr_two = 1.0 - 0.95**STEP
    wfloat = weight.astype(jnp.float32)
    update = new_first / corr_one / (jnp.sqrt(new_second / corr_two) + 1e-08) + 0.1 * wfloat
    return ((wfloat - 0.001 * update).astype(jnp.bfloat16), new_first, new_second)


def rows_product(left, rows):
    return lax.dot_general(left, rows, (((1,), (1,)), ((), ())), preferred_element_type=jnp.float32)


def local(hidden, gain, head_weight, first_moment, second_moment, targets):
    hfloat = hidden.astype(jnp.float32)
    scale = lax.rsqrt(jnp.mean(hfloat * hfloat, axis=-1, keepdims=True) + 1e-06)
    normed = (hfloat * scale * gain).astype(jnp.bfloat16)
    group = head_weight.shape[0] * lax.axis_size("dp")
    offset = lax.axis_index("vocab") * group
    block_rows = lax.all_gather(head_weight, "dp", axis=0, tiled=True)
    logits = rows_product(normed, block_rows)
    top = lax.pmax(jnp.max(logits, axis=-1, keepdims=True), "vocab")
    expo = jnp.exp(logits - top)
    total = lax.psum(jnp.sum(expo, axis=-1, keepdims=True), "vocab")
    columns = offset + jnp.arange(group, dtype=jnp.int32)
    onehot = (targets[:, None] == columns[None, :]).astype(jnp.float32)
    grad_logits = (expo / total - onehot).astype(jnp.bfloat16)
    partial_grad = jnp.dot(grad_logits, block_rows, preferred_element_type=jnp.float32)
    grad_normed = lax.psum(partial_grad, "vocab")
    scaled = grad_normed * gain
    dot_mean = jnp.mean(scaled * hfloat, axis=-1, keepdims=True)
    grad_hidden = (scale * scaled - hfloat * scale**3 * dot_mean).astype(jnp.bfloat16)
    grad_gain = lax.psum(jnp.sum(grad_normed * hfloat * scale, axis=0), "dp")
    grad_head = lax.psum_scatter(
        lax.dot_general(
            grad_logits, normed, (((0,), (0,)), ((), ())), preferred_element_type=jnp.float32
        ),
        "dp",
        scatter_dimension=0,
        tiled=True,
    )
    new_weight, new_first, new_second = adam_step(
        head_weight, first_moment, second_moment, grad_head
    )
    return (grad_hidden, grad_gain, new_weight, new_first, new_second)


def solution(mesh):
    placed = (
        P("dp", None),
        P(),
        P(("vocab", "dp"), None),
        P(("vocab", "dp"), None),
        P(("vocab", "dp"), None),
        P("dp"),
    )
    return jax.shard_map(
        local,
        mesh=mesh,
        in_specs=placed,
        out_specs=(
            P("dp", None),
            P(),
            P(("vocab", "dp"), None),
            P(("vocab", "dp"), None),
            P(("vocab", "dp"), None),
        ),
        check_vma=False,
    )
```

profile of v0, /device:TPU:1, one launch (start us, length us, event | category | flops | bytes accessed | tf_op | source)
XLA Modules:
  0.0 1339.4 jit_solution(7873236037831435260)
XLA Ops:
  7.2 0.0 copy-start
  7.2 0.0 copy-start.2
  7.2 0.0 all-gather.2.cloned.1.call-start
  7.2 0.7 all-gather.2.cloned.1.call-update
  7.9 0.0 all-reduce.2.cloned.1.call-start
  8.0 1.9 fusion
  9.9 400.6 %all-gather.2.cloned.1.call-done = bf16[2560,7168]{1,0:T(8,128)(2,1)} async-done(((bf16[80,7168]{1,0:T(8,128)(2,1)}), bf16[2560,7168]{1,0:T(8,128)(2,1)}) %all-gather.2.cloned.1.call-update) | async-done | bytes 36700176 | tf_op jit(solution)/shard_map/all_gather | solution.py:29
  410.5 0.0 copy-done
  410.5 0.0 copy-done.2
  410.5 17.4 %fusion.20 = (f32[128]{0:T(128)S(1)}, f32[128,2560]{1,0:T(8,128)S(1)}) fusion(bf16[2560,7168]{1,0:T(8,128)(2,1)} %all-gather.2.cloned.1.call-done, bf16[128,7168]{1,0:T(8,128)(2,1)S(1)} %copy-done, f32[7168]{0:T(1024)S(1)} %copy-done.2, f32[128]{0:T(128)S(1)} %get-tuple-element.11), kind=kOutput, calls=%fused_computation.32 | convolution fusion | flops 4701618176 | bytes 39875584 | tf_op jit(solution)/shard_map/dot_general | solution.py:20
  427.9 7.2 pmax.7
  435.2 0.3 fusion.13
  435.5 9.6 psum.21
  445.1 18.5 %fusion.18 = f32[128,7168]{1,0:T(8,128)} fusion(bf16[2560,7168]{1,0:T(8,128)(2,1)} %all-gather.2.cloned.1.call-done, f32[128,2560]{1,0:T(8,128)S(1)} %get-tuple-element.13, s32[2560]{0:T(1024)S(1)} %iota_add_fusion, f32[128]{0:T(128)S(1)} %psum.21, f32[128]{0:T(128)S(1)} %pmax.7, s32[128]{0:T(128)S(1)} %copy-done.3), kind=kOutput, calls=%fused_computation.31 | convolution fusion | flops 4699586560 | bytes 41692672 | tf_op jit(solution)/shard_map/dot_general | solution.py:37
  463.6 0.0 all-reduce.2.cloned.1.call-update
  463.7 0.2 reduce-scatter.2.cloned.1.call-start
  463.9 26.7 %fusion.14 = f32[2560,7168]{1,0:T(8,128)} fusion(bf16[128,7168]{1,0:T(8,128)(2,1)S(1)} %copy-done, f32[7168]{0:T(1024)S(1)} %copy-done.2, f32[128]{0:T(128)S(1)} %get-tuple-element.11, f32[128,2560]{1,0:T(8,128)S(1)} %get-tuple-element.13, s32[2560]{0:T(1024)S(1)} %iota_add_fusion, f32[128]{0:T(128)S(1)} %psum.21, f32[128]{0:T(128)S(1)} %pmax.7, ...), kind=kOutput, calls=%fused_computation.25 | convolution fusion | flops 4703256576 | bytes 76587008 | tf_op jit(solution)/shard_map/dot_general | solution.py:44
  490.6 0.0 reduce-scatter.2.cloned.1.call-update
  490.6 52.8 %all-reduce.2.cloned.1.call-done = f32[128,7168]{1,0:T(8,128)} async-done(((f32[128,7168]{1,0:T(8,128)}), f32[128,7168]{1,0:T(8,128)}) %all-reduce.2.cloned.1.call-update) | async-done | bytes 3670032 | tf_op jit(solution)/shard_map/psum | solution.py:38
  543.4 3.3 fusion.8
  546.8 148.4 %psum.23 = f32[7168]{0:T(1024)} all-reduce(f32[7168]{0:T(1024)S(1)} %get-tuple-element.5), channel_id=1, replica_groups=mesh['vocab'=4,'dp'=32] {'dp'}, use_global_device_ids=true, to_apply=%region_8.0 | all-reduce | flops 7168 | bytes 57344 | tf_op jit(solution)/shard_map/psum | solution.py:42
  695.2 4.5 fusion.5
  699.7 626.4 %reduce-scatter.2.cloned.1.call-done = f32[80,7168]{1,0:T(8,128)} async-done(((f32[2560,7168]{1,0:T(8,128)}), f32[80,7168]{1,0:T(8,128)}) %reduce-scatter.2.cloned.1.call-update) | async-done | bytes 2293776 | tf_op jit(solution)/shard_map/reduce_scatter | solution.py:43
  1326.1 6.8 fusion.11
  (7 shorter events, 0.0 us)
Async XLA Ops:
  7.2 403.3 %copy-start = (bf16[128,7168]{1,0:T(8,128)(2,1)S(1)}, bf16[128,7168]{1,0:T(8,128)(2,1)}, u32[]{:S(2)}) copy-start(bf16[128,7168]{1,0:T(8,128)(2,1)} %param.6) | copy-start | bytes 5505028
  7.2 403.3 %copy-start.2 = (f32[7168]{0:T(1024)S(1)}, f32[7168]{0:T(1024)}, u32[]{:S(2)}) copy-start(f32[7168]{0:T(1024)} %param.7) | copy-start | bytes 86020
  7.2 403.3 %all-gather.2.cloned.1.call-start = ((), (), s32[]{:S(2)}) async-start(), calls=%async_computation.1 | async-start | bytes 37847040 | tf_op jit(solution)/shard_map/all_gather | solution.py:29
  7.9 535.5 %all-reduce.2.cloned.1.call-start = ((), (), s32[]{:S(2)}) async-start(), calls=%async_computation.2 | async-start | bytes 7340032 | tf_op jit(solution)/shard_map/psum | solution.py:38
  410.5 34.6 %copy-start.3 = (s32[128]{0:T(128)S(1)}, s32[128]{0:T(128)}, u32[]{:S(2)}) copy-start(s32[128]{0:T(128)} %param.11) | copy-start | bytes 1540
  463.7 862.5 %reduce-scatter.2.cloned.1.call-start = ((), (), s32[]{:S(2)}) async-start(), calls=%async_computation.3 | async-start | bytes 75694080 | tf_op jit(solution)/shard_map/reduce_scatter | solution.py:43
  695.2 631.0 %copy-start.1 = (bf16[80,7168]{1,0:T(8,128)(2,1)S(1)}, bf16[80,7168]{1,0:T(8,128)(2,1)}, u32[]{:S(2)}) copy-start(bf16[80,7168]{1,0:T(8,128)(2,1)} %param.8) | copy-start | bytes 3440644
Sparse Core Ops, SparseCore 0:
  9.7 400.7 all-gather.1
  463.8 79.5 all-reduce.1
  545.9 780.1 reduce-scatter.1
where the time goes:
time: 1340 us
  waiting for transfers between devices  1080 us (81%)
  blocking collectives  165 us (12%)
  matrix products  62.6 us (5%)
  other arithmetic  16.9 us (1%)
  between operations  13.8 us (1%)
    reduce_scatter x1, waiting for transfers between devices, local(): lax.psum_scatter(lax.dot_general(grad_logits, normed, (((0,), (0,)), ((),...  626 us
    all_gather x1, waiting for transfers between devices, local(): block_rows = lax.all_gather(head_weight, 'dp', axis=0, tiled=True)  401 us
    psum x1, blocking collectives, local(): grad_gain = lax.psum(jnp.sum(grad_normed * hfloat * scale, axis=0), 'dp')  148 us
    psum x1, waiting for transfers between devices, local(): grad_normed = lax.psum(partial_grad, 'vocab')  52.8 us
  transfers between devices with their start and end apart: 3, of which 3 were waited for; matrix products, arithmetic and copies ran while one was open for 3% of the time, Pallas kernels for 0%

commit v1 on v0

v1 whole, which is shorter than its diff:
```python
import jax
import jax.numpy as jnp
from jax import lax
from jax.experimental import pallas as pl
from jax.experimental.pallas import tpu as pltpu
from jax.sharding import Mesh
from jax.sharding import PartitionSpec as P

STEP = 100
AXES = ("xh", "core", "xl", "z", "y")
SIZES = (2, 2, 2, 4, 4)
VMEM_LIMIT = 56 * 1024 * 1024
BLOCK = 1792
LANES = 128
half = jnp.bfloat16


def adam_step(weight, first, second, grads):
    new_first = 0.9 * first + 0.1 * grads
    new_second = 0.95 * second + 0.05 * grads * grads
    corr_one = 1.0 - 0.9**STEP
    corr_two = 1.0 - 0.95**STEP
    wfloat = weight.astype(jnp.float32)
    update = new_first / corr_one / (jnp.sqrt(new_second / corr_two) + 1e-08) + 0.1 * wfloat
    return ((wfloat - 0.001 * update).astype(jnp.bfloat16), new_first, new_second)


def place(x, core, z, y):
    index = 0
    for size, at in zip(SIZES, (x // 2, core, x % 2, z, y)):
        index = index * size + at
    return index


def move(array, step):
    pairs = []
    for x in range(4):
        for core in range(2):
            for z in range(4):
                for y in range(4):
                    x_to, core_to, z_to, y_to = step(x, core, z, y)
                    pairs.append((place(x, core, z, y), place(x_to % 4, core_to % 2, z_to % 4, y_to % 4)))
    return lax.ppermute(array, AXES, pairs)


def along_core(array):
    return move(array, lambda x, core, z, y: (x, core + 1, z, y))


def along_x(array, by):
    return move(array, lambda x, core, z, y: (x + by, core, z, y))


def flip_x(array):
    return move(array, lambda x, core, z, y: (x + 1 - 2 * core, core, z, y))


def along_y(array, by):
    return move(array, lambda x, core, z, y: (x, core, z, y + by * (1 - 2 * core)))


def along_z(array, by):
    return move(array, lambda x, core, z, y: (x, core, z + by * (1 - 2 * core), y))


def short(array):
    return array.astype(jnp.bfloat16)


def wide(array):
    return array.astype(jnp.float32)


def together(*arrays):
    return lax.optimization_barrier(arrays)


def merge(stats):
    top = jnp.max(stats[:, 0], axis=0)
    total = jnp.sum(stats[:, 1] * jnp.exp(stats[:, 0] - top), axis=0)
    return jnp.stack([top, total])


def strips(pieces):
    return [pl.BlockSpec((piece.shape[0], BLOCK), lambda i: (0, i)) for piece in pieces]


def whole(shape):
    return pl.BlockSpec(shape, lambda i: (0,) * len(shape))


def anywhere(arrays):
    return [pl.BlockSpec(memory_space=pl.ANY) for _ in arrays]


def params():
    return pltpu.CompilerParams(vmem_limit_bytes=VMEM_LIMIT)


def cost(rows, columns, depth):
    return pl.CostEstimate(
        flops=2 * rows * columns * depth, bytes_accessed=2 * depth * (rows + columns), transcendentals=0
    )


def by_strips(step, operands, outs, after=(), passed=()):
    width = operands[0][0].shape[1]
    block = 2 * BLOCK

    def kernel(*refs):
        taken = refs[: len(operands)]
        given = refs[len(operands) + len(after) + len(passed) :]
        for ref, value in zip(given, step(*[ref[...] for ref in taken])):
            ref[...] = value.astype(ref.dtype)

    def strip(rows, at=0):
        return pl.BlockSpec((rows, block), lambda i: (at, i))

    size = sum(rows for _, _, rows in operands) + sum(rows for rows, _ in outs)
    return pl.pallas_call(
        kernel,
        grid=(width // block,),
        in_specs=[strip(rows, start // rows) for _, start, rows in operands]
        + anywhere(after)
        + anywhere(passed),
        out_specs=[strip(rows) for rows, _ in outs] + anywhere(passed),
        out_shape=[jax.ShapeDtypeStruct((rows, width), dtype) for rows, dtype in outs]
        + [jax.ShapeDtypeStruct(array.shape, array.dtype) for array in passed],
        input_output_aliases={len(operands) + len(after) + i: len(outs) + i for i in range(len(passed))},
        compiler_params=params(),
        cost_estimate=pl.CostEstimate(flops=0, bytes_accessed=2 * size * width, transcendentals=0),
    )(*[array for array, _, _ in operands], *after, *passed)


def all_rows(*arrays):
    return [(array, 0, array.shape[0]) for array in arrays]


def norm_kernel(core_ref, hidden_ref, gain_ref, digits_ref, own_ref):
    width = hidden_ref.shape[1]
    hfloat = wide(hidden_ref[...])
    scale = lax.rsqrt(jnp.mean(hfloat * hfloat, axis=-1, keepdims=True) + 1e-06)
    own_ref[:, :width] = short(hfloat * scale * gain_ref[...])
    own_ref[:, width:] = digits_ref[...]


def normed_half(hidden, gain, digits, core):
    rows, width = hidden.shape
    block = rows // 4
    return pl.pallas_call(
        norm_kernel,
        grid_spec=pltpu.PrefetchScalarGridSpec(
            num_scalar_prefetch=1,
            grid=(2,),
            in_specs=[
                pl.BlockSpec((block, width), lambda i, core_ref: (core_ref[0] * 2 + i, 0)),
                pl.BlockSpec((1, width), lambda i, core_ref: (0, 0)),
                pl.BlockSpec((block, LANES), lambda i, core_ref: (core_ref[0] * 2 + i, 0)),
            ],
            out_specs=pl.BlockSpec((block, width + LANES), lambda i, core_ref: (i, 0)),
        ),
        out_shape=jax.ShapeDtypeStruct((rows // 2, width + LANES), half),
        compiler_params=params(),
        cost_estimate=pl.CostEstimate(flops=0, bytes_accessed=16 * rows * width, transcendentals=0),
    )(core.reshape(1), hidden, gain.reshape(1, width), digits)


def stack_of(refs):
    return jnp.concatenate([ref[...] for ref in refs], axis=0)


def logits_kernel(n_head, n_token, *refs):
    head = stack_of(refs[:n_head])
    tokens = stack_of(refs[n_head : n_head + n_token])
    digit_refs = refs[n_head + n_token : n_head + 2 * n_token]
    logits_ref, stats_ref = refs[-2:]
    product = lax.dot_general(head, tokens, (((1,), (1,)), ((), ())), preferred_element_type=jnp.float32)
    step = pl.program_id(0)

    @pl.when(step == 0)
    def _():
        logits_ref[...] = product

    @pl.when(step > 0)
    def _():
        logits_ref[...] += product

    @pl.when(step == pl.num_programs(0) - 1)
    def _():
        logits = logits_ref[...]
        top = jnp.max(logits, axis=0, keepdims=True)
        stats_ref[0:1, :] = top
        stats_ref[1:2, :] = jnp.sum(jnp.exp(logits - top), axis=0, keepdims=True)
        digits = wide(stack_of(digit_refs)).T
        stats_ref[2:3, :] = digits[0:1, :] * float(LANES) + digits[1:2, :]


def all_logits(head, tokens, after=()):
    rows, columns = (sum(piece.shape[0] for piece in pieces) for pieces in (head, tokens))
    width = head[0].shape[1]
    digits = [pl.BlockSpec((piece.shape[0], LANES), lambda i: (0, width // LANES)) for piece in tokens]
    return pl.pallas_call(
        lambda *refs: logits_kernel(len(head), len(tokens), *refs),
        grid=(width // BLOCK,),
        in_specs=strips(head) + strips(tokens) + digits + anywhere(after),
        out_specs=[whole((rows, columns)), whole((3, columns))],
        out_shape=[
            jax.ShapeDtypeStruct((rows, columns), jnp.float32),
            jax.ShapeDtypeStruct((3, columns), jnp.float32),
        ],
        compiler_params=params(),
        cost_estimate=cost(rows, columns, width),
    )(*head, *tokens, *tokens, *after)


def spread(product, outs, part):
    for k, ref in enumerate(outs):
        ref[...] = product[k * part : (k + 1) * part]


def token_grad_kernel(n_head, part, near_ref, flip_ref, stats_ref, wanted_ref, *refs):
    grads_ref = refs[n_head]
    outs, turned_ref = refs[n_head + 1 : -1], refs[-1]

    @pl.when(pl.program_id(0) == 0)
    def _():
        logits = jnp.concatenate([near_ref[...], flip_ref[...]], axis=1)
        rows = lax.broadcasted_iota(jnp.int32, logits.shape, 0)
        share = jnp.exp(logits - stats_ref[0:1, :]) / stats_ref[1:2, :]
        grads = share - jnp.where(rows == wanted_ref[...], 1.0, 0.0)
        grads_ref[...] = short(grads)
        turned_ref[...] = short(grads.T)

    product = jnp.dot(turned_ref[...], stack_of(refs[:n_head]), preferred_element_type=jnp.float32)
    spread(short(product), outs, part)


def token_grads(near, flip, stats, wanted, head):
    rows, columns = near.shape[0], near.shape[1] * 2
    width, part = head[0].shape[1], columns // 8
    return pl.pallas_call(
        lambda *refs: token_grad_kernel(len(head), part, *refs),
        grid=(width // BLOCK,),
        in_specs=[whole(near.shape), whole(flip.shape), whole((2, columns)), whole((1, columns))] + strips(head),
        out_specs=[whole((rows, columns))] + [pl.BlockSpec((part, BLOCK), lambda i: (0, i))] * 8,
        out_shape=[jax.ShapeDtypeStruct((rows, columns), half)] + [jax.ShapeDtypeStruct((part, width), half)] * 8,
        scratch_shapes=[pltpu.VMEM((columns, rows), half)],
        compiler_params=params(),
        cost_estimate=cost(rows, columns, width),
    )(near, flip, stats, wanted, *head)


def head_grad_kernel(n_head, n_token, grads_ref, *refs):
    near_ref, other_ref, gain_ref = refs[n_head + n_token :]
    tokens = stack_of(refs[n_head : n_head + n_token])
    product = jnp.dot(grads_ref[...], tokens, preferred_element_type=jnp.float32)
    rows = near_ref.shape[0]
    near_ref[...] = product[:rows]
    other_ref[...] = short(product[rows:])
    gain_ref[...] = jnp.sum(product * wide(stack_of(refs[:n_head])), axis=0, keepdims=True)


def head_grads(grads, head, tokens):
    rows, columns = grads.shape
    width = head[0].shape[1]
    return pl.pallas_call(
        lambda *refs: head_grad_kernel(len(head), len(tokens), *refs),
        grid=(width // BLOCK,),
        in_specs=[whole((rows, columns))] + strips(head) + strips(tokens),
        out_specs=[pl.BlockSpec((size, BLOCK), lambda i: (0, i)) for size in (rows // 2, rows // 2, 1)],
        out_shape=[
            jax.ShapeDtypeStruct((rows // 2, width), jnp.float32),
            jax.ShapeDtypeStruct((rows // 2, width), half),
            jax.ShapeDtypeStruct((1, width), jnp.float32),
        ],
        compiler_params=params(),
        cost_estimate=cost(rows, columns, width),
    )(grads, *head, *tokens)


def hidden_grad_kernel(core_ref, mine_ref, their_ref, hidden_ref, gain_ref, *refs):
    hfloat = wide(hidden_ref[...])
    scale = lax.rsqrt(jnp.mean(hfloat * hfloat, axis=-1, keepdims=True) + 1e-06)
    scaled = (wide(mine_ref[...]) + wide(their_ref[...])) * gain_ref[...]
    dot_mean = jnp.mean(scaled * hfloat, axis=-1, keepdims=True)
    refs[-1][...] = short(scale * scaled - hfloat * scale**3 * dot_mean)


def hidden_grads(mine, their, hidden, gain, core, after):
    rows, width = hidden.shape
    block = rows // 4
    return pl.pallas_call(
        hidden_grad_kernel,
        grid_spec=pltpu.PrefetchScalarGridSpec(
            num_scalar_prefetch=1,
            grid=(2,),
            in_specs=[
                pl.BlockSpec((block, width), lambda i, core_ref: (i, 0)),
                pl.BlockSpec((block, width), lambda i, core_ref: (i, 0)),
                pl.BlockSpec((block, width), lambda i, core_ref: (core_ref[0] * 2 + i, 0)),
                pl.BlockSpec((1, width), lambda i, core_ref: (0, 0)),
            ]
            + anywhere(after),
            out_specs=pl.BlockSpec((block, width), lambda i, core_ref: (i, 0)),
        ),
        out_shape=jax.ShapeDtypeStruct((rows // 2, width), half),
        compiler_params=params(),
        cost_estimate=pl.CostEstimate(flops=0, bytes_accessed=4 * rows * width, transcendentals=0),
    )(core.reshape(1), mine, their, hidden, gain.reshape(1, width), *after)


def local(hidden, gain, head_weight, first_moment, second_moment, targets):
    core = lax.axis_index("core")
    rows, width = hidden.shape
    held = head_weight.shape[0]
    part = rows // 2

    lane = lax.broadcasted_iota(jnp.int32, (rows, LANES), 1)
    wanted = targets[:, None]
    digits = jnp.where(lane == 0, wanted // LANES, jnp.where(lane == 1, wanted % LANES, 0)).astype(half)
    head_after, head_before = along_z(head_weight, -1), along_z(head_weight, 1)
    own = normed_half(hidden, gain, digits, core)
    own_after, own_before = along_y(own, -1), along_y(own, 1)
    flip_own = flip_x(own)
    own_after, own_before, flip_own = together(own_after, own_before, flip_own)
    own_far = along_y(own_after, -1)
    flip_after = flip_x(own_after)
    head_far = along_z(head_after, -1)
    other_own, other_after, other_before = (along_core(block) for block in (head_weight, head_after, head_before))
    own_far, flip_after = together(own_far, flip_after)
    flip_before = along_y(flip_own, 1)
    flip_far = flip_x(own_far)
    other_far = along_core(head_far)

    head = [head_weight, head_after, head_far, head_before, other_own, other_after, other_far, other_before]
    near_tokens = [own, own_after, own_far, own_before]
    flip_tokens = [flip_own, flip_after, flip_far, flip_before]
    near_logits, near_stats = all_logits(head, near_tokens)
    flip_logits, flip_stats = all_logits(head, flip_tokens, after=[near_stats])

    stats = jnp.stack([near_stats[:2], flip_stats[:2]], axis=1).reshape(2, 2, 4, part)
    stats = merge(jnp.stack([stats] + [jnp.roll(along_y(stats, by), -by, axis=2) for by in (1, 2, 3)]))
    stats = merge(jnp.stack([stats] + [jnp.roll(along_x(stats, by), by, axis=1) for by in (1, 2, 3)]))
    stats = stats.reshape(2, 8 * part)
    wanted = jnp.concatenate([near_stats[2:], flip_stats[2:]], axis=1).astype(jnp.int32)
    z, others = lax.axis_index("z"), lax.axis_index("xl") * 16 + lax.axis_index("y")
    spot = jnp.full_like(wanted, -1)
    for other in range(2):
        at_core = (core + other) % 2
        block = lax.axis_index("xh") * 2 + at_core
        for step in range(4):
            start = (block * 32 + others + (z + step * (1 - 2 * at_core)) % 4 * 4) * held
            inside = (wanted >= start) & (wanted < start + held)
            spot = jnp.where(inside, wanted - start + (other * 4 + step) * held, spot)

    grads, sum_own, sum_after, sum_far, sum_before, flip_own, flip_after, flip_far, flip_before = token_grads(
        near_logits, flip_logits, stats, spot, head
    )
    flip_far = flip_x(flip_far)
    flip_before = along_y(flip_before, -1)
    near_head, other_head, gain_sum = head_grads(grads, head, near_tokens + flip_tokens)

    sum_far, gain_sum, other_head, flip_after, sum_before = by_strips(
        lambda far, f_far, g_sum: (wide(far) + wide(f_far), g_sum),
        all_rows(sum_far, flip_far, gain_sum),
        [(part, half), (1, jnp.float32)],
        after=[flip_before],
        passed=[other_head, flip_after, sum_before],
    )
    sum_far = along_y(sum_far, 1)
    flip_after = flip_x(flip_after)
    other_head = along_core(other_head)
    sum_before = along_y(sum_before, -1)
    gain_sum = gain_sum + move(gain_sum, lambda x, core, z, y: (x, core, z ^ 1, y))
    gain_other = move(gain_sum, lambda x, core, z, y: (x, core, z + 2, y))
    head_far, head_before, gain_sum = by_strips(
        lambda mine, theirs, mine_too, theirs_too, g_sum, g_other: (
            mine + wide(theirs),
            mine_too + wide(theirs_too),
            g_sum + g_other,
        ),
        [(near_head, 2 * held, held), (other_head, 2 * held, held)]
        + [(near_head, 3 * held, held), (other_head, 3 * held, held)]
        + all_rows(gain_sum, gain_other),
        [(held, half), (held, half), (1, jnp.float32)],
    )

    sum_after, flip_own, head_far, head_before, gain_sum = by_strips(
        lambda after, f_after, far, own, before: (wide(after) + wide(f_after) + wide(far), wide(own) + wide(before)),
        all_rows(sum_after, flip_after, sum_far, flip_own, flip_before),
        [(part, half), (part, half)],
        after=[sum_before],
        passed=[head_far, head_before, gain_sum],
    )
    sum_after = along_y(sum_after, 1)
    flip_own = flip_x(flip_own)
    head_far, head_before = along_z(head_far, 1), along_z(head_before, -1)
    gain_sum = gain_sum + along_core(gain_sum)
    gain_other = move(gain_sum, lambda x, core, z, y: (x ^ 1, core, z, y))

    summed, gain_sum = by_strips(
        lambda a, b, c, d, mine, theirs: (wide(a) + wide(b) + (wide(c) + wide(d)), mine + theirs),
        all_rows(sum_own, flip_own, sum_after, sum_before, gain_sum, gain_other),
        [(part, half), (1, jnp.float32)],
    )
    (head_after,) = by_strips(
        lambda mine, theirs, far: (mine + wide(theirs) + wide(far),),
        [(near_head, held, held), (other_head, held, held), (head_far, 0, held)],
        [(held, half)],
        after=[summed],
    )
    head_after = along_z(head_after, 1)
    grad_hidden = hidden_grads(summed, along_x(summed, 2), hidden, gain, core, [head_after])
    other_half = along_core(grad_hidden)
    grad_hidden = jnp.where(
        core == 0,
        jnp.concatenate([grad_hidden, other_half]),
        jnp.concatenate([other_half, grad_hidden]),
    )

    gain_sum = gain_sum + move(gain_sum, lambda x, core, z, y: (x, core, z, y ^ 1))
    gain_sum = gain_sum + move(gain_sum, lambda x, core, z, y: (x, core, z, y + 2))
    grad_gain = gain_sum + along_x(gain_sum, 2)
    grad_gain = grad_gain.reshape(width) / gain

    grad_head = near_head[:held] + wide(other_head[:held]) + wide(head_after) + wide(head_before)
    new_weight, new_first, new_second = adam_step(head_weight, first_moment, second_moment, grad_head)
    return (grad_hidden, grad_gain, new_weight, new_first, new_second)


def solution(mesh):
    fine = Mesh(mesh.devices.reshape(SIZES), AXES)
    dp = ("xl", "z", "y")
    rows = P(AXES, None)
    return jax.shard_map(
        local,
        mesh=fine,
        in_specs=(P(dp, None), P(), rows, rows, rows, P(dp)),
        out_specs=(P(dp, None), P(), rows, rows, rows),
        check_vma=False,
    )
```

time: 1340 us -> 220 us (0.16)
  waiting for transfers between devices: 1080 us -> 68 us
  blocking collectives: 165 us -> 0 us
  starting transfers between devices: 0.3 us -> 63.2 us
  matrix products: 62.6 us -> 0 us
  Pallas kernels: 0 us -> 61.5 us
  local copies, waits for them, and re-layouts: 0.02 us -> 13.5 us
    reduce_scatter x1 -> x0, waiting for transfers between devices: 626 us -> none  [local(): lax.psum_scatter(lax.dot_general(grad_logits, normed, (((0,), (0,)), ((),...]
    all_gather x1 -> x0, waiting for transfers between devices: 401 us -> none  [local(): block_rows = lax.all_gather(head_weight, 'dp', axis=0, tiled=True)]
    psum x2 -> x0, blocking collectives: 158 us -> none  [the longest x1 148 us: local(): grad_gain = lax.psum(jnp.sum(grad_normed * hfloat * scale, axis=0), 'dp')]
    ppermute x0 -> x40, waiting for transfers between devices: none -> 68 us  [move(): return lax.ppermute(array, AXES, pairs)]
    ppermute x0 -> x40, starting transfers between devices: none -> 63.2 us  [move(): return lax.ppermute(array, AXES, pairs)]
    dot_general x3 -> x0, matrix products: 62.6 us -> none  [the longest x1 26.7 us: local(): lax.dot_general(grad_logits, normed, (((0,), (0,)), ((), ())), preferred_...]
    pallas_call x0 -> x11, Pallas kernels: none -> 61.5 us  [the longest x5 16.3 us: by_strips(): pl.pallas_call(kernel, grid=(width // block,), in_specs=[strip(rows, star...]
    psum x1 -> x0, waiting for transfers between devices: 52.8 us -> none  [local(): grad_normed = lax.psum(partial_grad, 'vocab')]
  transfers between devices with their start and end apart: 3 -> 40, of which waited for: 3 -> 20; matrix products, arithmetic and copies ran while one was open for 3% -> 5% of each run, Pallas kernels for 0% -> 15%
where the time goes in v1:
time: 220 us; the launch traced here: 219 us
  waiting for transfers between devices  68 us (31%)
  starting transfers between devices  63.2 us (29%)
  Pallas kernels  61.5 us (28%)
  local copies, waits for them, and re-layouts  13.5 us (6%)
  other arithmetic  11.9 us (5%)
    ppermute x40, waiting for transfers between devices, move(): return lax.ppermute(array, AXES, pairs)  68 us
    ppermute x40, starting transfers between devices, move(): return lax.ppermute(array, AXES, pairs)  63.2 us
    pallas_call x5, Pallas kernels, by_strips(): pl.pallas_call(kernel, grid=(width // block,), in_specs=[strip(rows, star...  16.3 us
    pallas_call x2, Pallas kernels, all_logits(): pl.pallas_call(lambda *refs: logits_kernel(len(head), len(tokens), *refs)...  15.5 us
    pallas_call x1, Pallas kernels, head_grads(): pl.pallas_call(lambda *refs: head_grad_kernel(len(head), len(tokens), *re...  12.8 us
    pallas_call x1, Pallas kernels, token_grads(): pl.pallas_call(lambda *refs: token_grad_kernel(len(head), part, *refs), g...  11.2 us
    unnamed x59, local copies, waits for them, and re-layouts  10.2 us
    convert_element_type x1, other arithmetic, adam_step(): (wfloat - 0.001 * update).astype(jnp.bfloat16)  5.29 us
  transfers between devices with their start and end apart: 40, of which 20 were waited for; matrix products, arithmetic and copies ran while one was open for 5% of the time, Pallas kernels for 15%

profile of v1, /device:TPU:1, one launch (start us, length us, event | category | flops | bytes accessed | tf_op | source)
XLA Modules:
  0.0 219.0 jit_solution(5300653366345790337)
XLA Ops:
  14.4 4.8 %collective-permute-done.refs_1_.refs_5_.refs_2_ = bf16[80,7168]{1,0:T(8,128)(2,1)S(1)} collective-permute-done((bf16[80,7168]{1,0:T(8,128)(2,1)}, bf16[80,7168]{1,0:T(8,128)(2,1)S(1)}, u32[]{:S(2)}, u32[]{:S(2)}) %collective-permute-start) | collective-permute-done | bytes 1146912 | tf_op jit(solution)/shard_map/ppermute | solution.py:43
  20.8 3.9 %collective-permute-done.7.refs_9_.refs_13_.refs_10_ = bf16[64,7296]{1,0:T(8,128)(2,1)S(1)} collective-permute-done((bf16[64,7296]{1,0:T(8,128)(2,1)}, bf16[64,7296]{1,0:T(8,128)(2,1)S(1)}, u32[]{:S(2)}, u32[]{:S(2)}) %collective-permute-start.7) | collective-permute-done | bytes 933920 | tf_op jit(solution)/shard_map/ppermute | solution.py:43
  24.7 4.3 %collective-permute-done.8.refs_11_.refs_15_.refs_12_ = bf16[64,7296]{1,0:T(8,128)(2,1)S(1)} collective-permute-done((bf16[64,7296]{1,0:T(8,128)(2,1)}, bf16[64,7296]{1,0:T(8,128)(2,1)S(1)}, u32[]{:S(2)}, u32[]{:S(2)}) %collective-permute-start.8) | collective-permute-done | bytes 933920 | tf_op jit(solution)/shard_map/ppermute | solution.py:43
  31.1 4.4 %collective-permute-start.3 = (bf16[80,7168]{1,0:T(8,128)(2,1)S(1)}, bf16[80,7168]{1,0:T(8,128)(2,1)S(1)}, u32[]{:S(2)}, u32[]{:S(2)}) collective-permute-start(bf16[80,7168]{1,0:T(8,128)(2,1)S(1)} %copy-done.1), channel_id=1, source_target_pairs={{0,32},{1,33},{2,34},{3,35},{4,36},{5,37},{6,38},{7,39},{8,40},{9,... | collective-permute-start | bytes 3440648 | tf_op jit(solution)/shard_map/ppermute | solution.py:43
  38.5 5.3 %collective-permute-done.10.refs_10_.refs_14_.refs_11_ = bf16[64,7296]{1,0:T(8,128)(2,1)} collective-permute-done((bf16[64,7296]{1,0:T(8,128)(2,1)S(1)}, bf16[64,7296]{1,0:T(8,128)(2,1)}, u32[]{:S(2)}, u32[]{:S(2)}) %collective-permute-start.10) | collective-permute-done | bytes 933920 | tf_op jit(solution)/shard_map/ppermute | solution.py:43
  53.7 7.8 %shard_map.102 = (f32[640,256]{1,0:T(8,128)}, f32[3,256]{1,0:T(4,128)}) custom-call(bf16[80,7168]{1,0:T(8,128)(2,1)} %refs_1_.1, bf16[80,7168]{1,0:T(8,128)(2,1)} %copy-done.3, bf16[80,7168]{1,0:T(8,128)(2,1)} %collective-permute-done.1.refs_2_.refs_6_.refs_3_, bf16[80,7168]{1,0:T(8,128)(2,1)} %copy-done.4, bf16[80,7168]{1,0:T(8,128)(2,1)} %copy-done.5, ...), custom_call_target="tpu_custom_call" | custom-call | flops 2348810240 | bytes 12845056 | tf_op jit(solution)/shard_map/pallas_call | solution.py:202
  65.5 7.7 %shard_map.103 = (f32[640,256]{1,0:T(8,128)}, f32[3,256]{1,0:T(4,128)}) custom-call(bf16[80,7168]{1,0:T(8,128)(2,1)} %refs_1_.1, bf16[80,7168]{1,0:T(8,128)(2,1)} %copy-done.3, bf16[80,7168]{1,0:T(8,128)(2,1)} %collective-permute-done.1.refs_2_.refs_6_.refs_3_, bf16[80,7168]{1,0:T(8,128)(2,1)} %copy-done.4, bf16[80,7168]{1,0:T(8,128)(2,1)} %copy-done.5, ...), custom_call_target="tpu_custom_call" | custom-call | flops 2348810240 | bytes 12845056 | tf_op jit(solution)/shard_map/pallas_call | solution.py:202
  82.4 2.8 %collective-permute-start.19 = (f32[2,2,4,64]{3,2,1,0:T(4,128)S(1)}, f32[2,2,4,64]{3,2,1,0:T(4,128)S(1)}, u32[]{:S(2)}, u32[]{:S(2)}) collective-permute-start(f32[2,2,4,64]{3,2,1,0:T(4,128)S(1)} %get-tuple-element.81), channel_id=1, source_target_pairs={{0,80},{1,81},{2,82},{3,83},{4,84},{5,85},{6,86},{7,87},{8,88},{9,... | collective-permute-start | bytes 12296 | tf_op jit(solution)/shard_map/ppermute | solution.py:43
  86.4 2.8 %collective-permute-done.18 = f32[2,2,4,64]{3,2,1,0:T(4,128)S(1)} collective-permute-done((f32[2,2,4,64]{3,2,1,0:T(4,128)S(1)}, f32[2,2,4,64]{3,2,1,0:T(4,128)S(1)}, u32[]{:S(2)}, u32[]{:S(2)}) %collective-permute-start.18) | collective-permute-done | bytes 4128 | tf_op jit(solution)/shard_map/ppermute | solution.py:43
  90.0 11.2 %shard_map.104 = (bf16[640,512]{1,0:T(8,128)(2,1)}, bf16[64,7168]{1,0:T(8,128)(2,1)}, bf16[64,7168]{1,0:T(8,128)(2,1)}, bf16[64,7168]{1,0:T(8,128)(2,1)}, bf16[6...) custom-call(f32[640,256]{1,0:T(8,128)} %get-tuple-element.44.refs_0_, ...), custom_call_target="tpu_custom_call" | custom-call | flops 4697620480 | bytes 16515072 | tf_op jit(solution)/shard_map/pallas_call | solution.py:241
  102.8 12.8 %shard_map.105 = (f32[320,7168]{1,0:T(8,128)}, bf16[320,7168]{1,0:T(8,128)(2,1)}, f32[1,7168]{1,0:T(1,128)}) custom-call(bf16[640,512]{1,0:T(8,128)(2,1)} %get-tuple-element.54.refs_0_, bf16[80,7168]{1,0:T(8,128)(2,1)} %refs_1_.1, bf16[80,7168]{1,0:T(8,128)(2,1)} %copy-done.3, bf16[80,7168]{1,0:T(8,128)(2,1)} %collective-permute-done.1.refs_2_.refs_6_.refs_3_, ...), custom_call_target="tpu_custom_call" | custom-call | flops 4697620480 | bytes 16515072 | tf_op jit(solution)/shard_map/pallas_call | solution.py:266
  120.0 5.3 %collective-permute-start.25 = (bf16[320,7168]{1,0:T(8,128)(2,1)}, bf16[320,7168]{1,0:T(8,128)(2,1)S(1)}, u32[]{:S(2)}, u32[]{:S(2)}) collective-permute-start(bf16[320,7168]{1,0:T(8,128)(2,1)} %get-tuple-element.65), channel_id=1, source_target_pairs={{0,32},{1,33},{2,34},{3,35},{4,36},{5,37},{6,38},{7,39},{8,40},{9,... | collective-permute-start | bytes 13762568 | tf_op jit(solution)/shard_map/ppermute | solution.py:43
  133.1 3.6 %collective-permute-start.27 = (f32[1,7168]{1,0:T(1,128)S(1)}, f32[1,7168]{1,0:T(1,128)S(1)}, u32[]{:S(2)}, u32[]{:S(2)}) collective-permute-start(f32[1,7168]{1,0:T(1,128)S(1)} %add.317.refs_4_), channel_id=1, source_target_pairs={{0,8},{1,9},{2,10},{3,11},{4,12},{5,13},{6,14},{7,15},{8,0},{9,1},... | collective-permute-start | bytes 86024 | tf_op jit(solution)/shard_map/ppermute | solution.py:43
  140.2 4.2 %shard_map.107 = (bf16[80,7168]{1,0:T(8,128)(2,1)}, bf16[80,7168]{1,0:T(8,128)(2,1)}, f32[1,7168]{1,0:T(1,128)}) custom-call(f32[320,7168]{1,0:T(8,128)} %get-tuple-element.64.refs_0_.refs_2_, bf16[320,7168]{1,0:T(8,128)(2,1)} %copy-done, f32[320,7168]{1,0:T(8,128)} %get-tuple-element.64.refs_0_.refs_2_, bf16[320,7168]{1,0:T(8,128)(2,1)} %copy-done, ...), custom_call_target="tpu_custom_call" | custom-call | bytes 6924288 | tf_op jit(solution)/shard_map/pallas_call | solution.py:120
  144.4 5.0 %collective-permute-done.23.refs_2_ = bf16[64,7168]{1,0:T(8,128)(2,1)S(1)} collective-permute-done((bf16[64,7168]{1,0:T(8,128)(2,1)}, bf16[64,7168]{1,0:T(8,128)(2,1)S(1)}, u32[]{:S(2)}, u32[]{:S(2)}) %collective-permute-start.23) | collective-permute-done | bytes 917536 | tf_op jit(solution)/shard_map/ppermute | solution.py:43
  150.6 3.4 %shard_map.108 = (bf16[64,7168]{1,0:T(8,128)(2,1)}, bf16[64,7168]{1,0:T(8,128)(2,1)}, bf16[80,7168]{1,0:T(8,128)(2,1)}, bf16[80,7168]{1,0:T(8,128)(2,1)}, f32[1,7168]{1,0:T(1,128)}) custom-call(bf16[64,7168]{1,0:T(8,128)(2,1)} %get-tuple-element.51.refs_0_, bf16[64,7168]{1,0:T(8,128)(2,1)} %copy-done.21, ...), custom_call_target="tpu_custom_call", output_to_operand_aliasing={{2}: (6, {}), {3}: (7, {}), {4}: (8, {})} | custom-call | bytes 6422528 | tf_op jit(solution)/shard_map/pallas_call | solution.py:120
  163.2 6.4 %collective-permute-done.31.refs_5_ = f32[1,7168]{1,0:T(1,128)S(1)} collective-permute-done((f32[1,7168]{1,0:T(1,128)S(1)}, f32[1,7168]{1,0:T(1,128)S(1)}, u32[]{:S(2)}, u32[]{:S(2)}) %collective-permute-start.31) | collective-permute-done | bytes 28704 | tf_op jit(solution)/shard_map/ppermute | solution.py:43
  172.3 3.1 %shard_map.109 = (bf16[64,7168]{1,0:T(8,128)(2,1)}, f32[1,7168]{1,0:T(1,128)}) custom-call(bf16[64,7168]{1,0:T(8,128)(2,1)} %get-tuple-element.50.refs_0_, bf16[64,7168]{1,0:T(8,128)(2,1)} %copy-done.19, bf16[64,7168]{1,0:T(8,128)(2,1)} %copy-done.20, bf16[64,7168]{1,0:T(8,128)(2,1)} %copy-done.12, f32[1,7168]{1,0:T(1,128)} %copy-done.24, f32[1,7168]{1,0:T(1,128)} %copy-done.26), custom_call_target="tpu_custom_call" | custom-call | bytes 4630528 | tf_op jit(solution)/shard_map/pallas_call | solution.py:120
  176.4 3.3 %shard_map.110 = bf16[80,7168]{1,0:T(8,128)(2,1)} custom-call(f32[320,7168]{1,0:T(8,128)} %get-tuple-element.64.refs_0_.refs_2_, bf16[320,7168]{1,0:T(8,128)(2,1)} %copy-done, bf16[80,7168]{1,0:T(8,128)(2,1)} %copy-done.17, bf16[64,7168]{1,0:T(8,128)(2,1)} %get-tuple-element.73.refs_3_.mine_ref), custom_call_target="tpu_custom_call" | custom-call | bytes 4587520 | tf_op jit(solution)/shard_map/pallas_call | solution.py:120
  182.2 3.1 %collective-permute-done.36 = f32[1,7168]{1,0:T(1,128)S(1)} collective-permute-done((f32[1,7168]{1,0:T(1,128)S(1)}, f32[1,7168]{1,0:T(1,128)S(1)}, u32[]{:S(2)}, u32[]{:S(2)}) %collective-permute-start.36) | collective-permute-done | bytes 28704 | tf_op jit(solution)/shard_map/ppermute | solution.py:43
  186.2 3.8 %collective-permute-done.37 = f32[1,7168]{1,0:T(1,128)S(1)} collective-permute-done((f32[1,7168]{1,0:T(1,128)S(1)}, f32[1,7168]{1,0:T(1,128)S(1)}, u32[]{:S(2)}, u32[]{:S(2)}) %collective-permute-start.37) | collective-permute-done | bytes 28704 | tf_op jit(solution)/shard_map/ppermute | solution.py:43
  191.6 11.7 %collective-permute-done.38 = f32[1,7168]{1,0:T(1,128)S(1)} collective-permute-done((f32[1,7168]{1,0:T(1,128)S(1)}, f32[1,7168]{1,0:T(1,128)S(1)}, u32[]{:S(2)}, u32[]{:S(2)}) %collective-permute-start.38) | collective-permute-done | bytes 28704 | tf_op jit(solution)/shard_map/ppermute | solution.py:43
  206.2 3.3 %shard_map.111 = bf16[64,7168]{1,0:T(8,128)(2,1)} custom-call(s32[1]{0:T(128)} %bitcast.core_ref, bf16[64,7168]{1,0:T(8,128)(2,1)} %get-tuple-element.73.refs_3_.mine_ref, bf16[64,7168]{1,0:T(8,128)(2,1)} %collective-permute-done.32.their_ref, bf16[128,7168]{1,0:T(8,128)(2,1)} %hidden_ref.3, f32[1,7168]{1,0:T(1,128)} %bitcast.50, bf16[80,7168]{1,0:T(8,128)(2,1)} %copy-done.6), custom_call_target="tpu_custom_call" | custom-call | bytes 3670016 | tf_op jit(solution)/shard_map/pallas_call | solution.py:292
  212.1 5.3 %fusion.2 = (bf16[80,7168]{1,0:T(8,128)(2,1)}, f32[80,7168]{1,0:T(8,128)}, f32[80,7168]{1,0:T(8,128)}) fusion(bf16[80,7168]{1,0:T(8,128)(2,1)S(1)} %copy-done.2, bf16[80,7168]{1,0:T(8,128)(2,1)} %collective-permute-done.39, bf16[80,7168]{1,0:T(8,128)(2,1)} %copy-done.6, bf16[320,7168]{1,0:T(8,128)(2,1)} %copy-done, ...), kind=kLoop, calls=%fused_computation.5 | loop fusion | flops 13189120 | bytes 17203200 | tf_op jit(solution)/shard_map/convert_element_type | solution.py:25
  (168 shorter events, 88.9 us)
Async XLA Ops:
  0.6 18.6 %collective-permute-start = (bf16[80,7168]{1,0:T(8,128)(2,1)}, bf16[80,7168]{1,0:T(8,128)(2,1)S(1)}, u32[]{:S(2)}, u32[]{:S(2)}) collective-permute-start(bf16[80,7168]{1,0:T(8,128)(2,1)} %refs_1_.1), channel_id=1, source_target_pairs={{0,12},{1,13},{2,14},{3,15},{4,0},{5,1},{6,2},{7,3},{8,4},{9,5},{1... | collective-permute-start | bytes 3440648 | tf_op jit(solution)/shard_map/ppermute | solution.py:43
  6.9 17.8 %collective-permute-start.7 = (bf16[64,7296]{1,0:T(8,128)(2,1)}, bf16[64,7296]{1,0:T(8,128)(2,1)S(1)}, u32[]{:S(2)}, u32[]{:S(2)}) collective-permute-start(bf16[64,7296]{1,0:T(8,128)(2,1)} %shard_map.101.refs_8_.refs_12_.refs_9_), channel_id=1, source_target_pairs={{0,3},{1,0},{2,1},{3,2},{4,7},{5,4},{6,5},{7,6},{8,11},{9,8},{10,9... | collective-permute-start | bytes 2801672 | tf_op jit(solution)/shard_map/ppermute | solution.py:43
  8.2 20.7 %collective-permute-start.8 = (bf16[64,7296]{1,0:T(8,128)(2,1)}, bf16[64,7296]{1,0:T(8,128)(2,1)S(1)}, u32[]{:S(2)}, u32[]{:S(2)}) collective-permute-start(bf16[64,7296]{1,0:T(8,128)(2,1)} %shard_map.101.refs_8_.refs_12_.refs_9_), channel_id=1, source_target_pairs={{0,1},{1,2},{2,3},{3,0},{4,5},{5,6},{6,7},{7,4},{8,9},{9,10},{10,1... | collective-permute-start | bytes 2801672 | tf_op jit(solution)/shard_map/ppermute | solution.py:43
  9.7 19.3 %collective-permute-start.9 = (bf16[64,7296]{1,0:T(8,128)(2,1)}, bf16[64,7296]{1,0:T(8,128)(2,1)}, u32[]{:S(2)}, u32[]{:S(2)}) collective-permute-start(bf16[64,7296]{1,0:T(8,128)(2,1)} %shard_map.101.refs_8_.refs_12_.refs_9_), channel_id=1, source_target_pairs={{0,16},{1,17},{2,18},{3,19},{4,20},{5,21},{6,22},{7,23},{8,24},{9,... | collective-permute-start | bytes 2801672 | tf_op jit(solution)/shard_map/ppermute | solution.py:43
  12.2 25.8 %collective-permute-start.2 = (bf16[80,7168]{1,0:T(8,128)(2,1)S(1)}, bf16[80,7168]{1,0:T(8,128)(2,1)S(1)}, u32[]{:S(2)}, u32[]{:S(2)}) collective-permute-start(bf16[80,7168]{1,0:T(8,128)(2,1)S(1)} %copy-done.1), channel_id=1, source_target_pairs={{0,4},{1,5},{2,6},{3,7},{4,8},{5,9},{6,10},{7,11},{8,12},{9,13},{1... | collective-permute-start | bytes 3440648 | tf_op jit(solution)/shard_map/ppermute | solution.py:43
  19.2 27.3 %collective-permute-start.1 = (bf16[80,7168]{1,0:T(8,128)(2,1)S(1)}, bf16[80,7168]{1,0:T(8,128)(2,1)}, u32[]{:S(2)}, u32[]{:S(2)}) collective-permute-start(bf16[80,7168]{1,0:T(8,128)(2,1)S(1)} %collective-permute-done.refs_1_.refs_5_.refs_2_), channel_id=1, source_target_pairs={{0,12},{1,13},{2,14},{3,15},{4,0},{5,1},{6,2},{7,3},{8,4},{9,5},{1... | collective-permute-start | bytes 3440648 | tf_op jit(solution)/shard_map/ppermute | solution.py:43
  29.9 13.9 %collective-permute-start.10 = (bf16[64,7296]{1,0:T(8,128)(2,1)S(1)}, bf16[64,7296]{1,0:T(8,128)(2,1)}, u32[]{:S(2)}, u32[]{:S(2)}) collective-permute-start(bf16[64,7296]{1,0:T(8,128)(2,1)S(1)} %collective-permute-done.7.refs_9_.refs_13_.refs_10_), channel_id=1, source_target_pairs={{0,3},{1,0},{2,1},{3,2},{4,7},{5,4},{6,5},{7,6},{8,11},{9,8},{10,9... | collective-permute-start | bytes 2801672 | tf_op jit(solution)/shard_map/ppermute | solution.py:43
  31.1 19.1 %collective-permute-start.3 = (bf16[80,7168]{1,0:T(8,128)(2,1)S(1)}, bf16[80,7168]{1,0:T(8,128)(2,1)S(1)}, u32[]{:S(2)}, u32[]{:S(2)}) collective-permute-start(bf16[80,7168]{1,0:T(8,128)(2,1)S(1)} %copy-done.1), channel_id=1, source_target_pairs={{0,32},{1,33},{2,34},{3,35},{4,36},{5,37},{6,38},{7,39},{8,40},{9,... | collective-permute-start | bytes 3440648 | tf_op jit(solution)/shard_map/ppermute | solution.py:43
  35.5 13.0 %collective-permute-start.11 = (bf16[64,7296]{1,0:T(8,128)(2,1)S(1)}, bf16[64,7296]{1,0:T(8,128)(2,1)S(1)}, u32[]{:S(2)}, u32[]{:S(2)}) collective-permute-start(bf16[64,7296]{1,0:T(8,128)(2,1)S(1)} %collective-permute-done.7.refs_9_.refs_13_.refs_10_), channel_id=1, source_target_pairs={{0,16},{1,17},{2,18},{3,19},{4,20},{5,21},{6,22},{7,23},{8,24},{9,... | collective-permute-start | bytes 2801672 | tf_op jit(solution)/shard_map/ppermute | solution.py:43
  37.9 15.7 %collective-permute-start.4 = (bf16[80,7168]{1,0:T(8,128)(2,1)S(1)}, bf16[80,7168]{1,0:T(8,128)(2,1)}, u32[]{:S(2)}, u32[]{:S(2)}) collective-permute-start(bf16[80,7168]{1,0:T(8,128)(2,1)S(1)} %collective-permute-done.refs_1_.refs_5_.refs_2_), channel_id=1, source_target_pairs={{0,32},{1,33},{2,34},{3,35},{4,36},{5,37},{6,38},{7,39},{8,40},{9,... | collective-permute-start | bytes 3440648 | tf_op jit(solution)/shard_map/ppermute | solution.py:43
  48.5 13.7 %collective-permute-start.13 = (bf16[64,7296]{1,0:T(8,128)(2,1)}, bf16[64,7296]{1,0:T(8,128)(2,1)}, u32[]{:S(2)}, u32[]{:S(2)}) collective-permute-start(bf16[64,7296]{1,0:T(8,128)(2,1)} %collective-permute-done.9.refs_8_.refs_12_.refs_13_), channel_id=1, source_target_pairs={{0,1},{1,2},{2,3},{3,0},{4,5},{5,6},{6,7},{7,4},{8,9},{9,10},{10,1... | collective-permute-start | bytes 2801672 | tf_op jit(solution)/shard_map/ppermute | solution.py:43
  51.2 13.3 %collective-permute-start.12 = (bf16[64,7296]{1,0:T(8,128)(2,1)}, bf16[64,7296]{1,0:T(8,128)(2,1)S(1)}, u32[]{:S(2)}, u32[]{:S(2)}) collective-permute-start(bf16[64,7296]{1,0:T(8,128)(2,1)} %collective-permute-done.10.refs_10_.refs_14_.refs_11_), channel_id=1, source_target_pairs={{0,16},{1,17},{2,18},{3,19},{4,20},{5,21},{6,22},{7,23},{8,24},{9,... | collective-permute-start | bytes 2801672 | tf_op jit(solution)/shard_map/ppermute | solution.py:43
  101.2 14.4 %collective-permute-start.20 = (bf16[64,7168]{1,0:T(8,128)(2,1)}, bf16[64,7168]{1,0:T(8,128)(2,1)S(1)}, u32[]{:S(2)}, u32[]{:S(2)}) collective-permute-start(bf16[64,7168]{1,0:T(8,128)(2,1)} %get-tuple-element.53), channel_id=1, source_target_pairs={{0,16},{1,17},{2,18},{3,19},{4,20},{5,21},{6,22},{7,23},{8,24},{9,... | collective-permute-start | bytes 2752520 | tf_op jit(solution)/shard_map/ppermute | solution.py:43
  102.8 14.0 %collective-permute-start.21 = (bf16[64,7168]{1,0:T(8,128)(2,1)}, bf16[64,7168]{1,0:T(8,128)(2,1)S(1)}, u32[]{:S(2)}, u32[]{:S(2)}) collective-permute-start(bf16[64,7168]{1,0:T(8,128)(2,1)} %get-tuple-element.56), channel_id=1, source_target_pairs={{0,3},{1,0},{2,1},{3,2},{4,7},{5,4},{6,5},{7,6},{8,11},{9,8},{10,9... | collective-permute-start | bytes 2752520 | tf_op jit(solution)/shard_map/ppermute | solution.py:43
  120.0 18.0 %collective-permute-start.25 = (bf16[320,7168]{1,0:T(8,128)(2,1)}, bf16[320,7168]{1,0:T(8,128)(2,1)S(1)}, u32[]{:S(2)}, u32[]{:S(2)}) collective-permute-start(bf16[320,7168]{1,0:T(8,128)(2,1)} %get-tuple-element.65), channel_id=1, source_target_pairs={{0,32},{1,33},{2,34},{3,35},{4,36},{5,37},{6,38},{7,39},{8,40},{9,... | collective-permute-start | bytes 13762568 | tf_op jit(solution)/shard_map/ppermute | solution.py:43
  125.3 19.1 %collective-permute-start.22 = (bf16[64,7168]{1,0:T(8,128)(2,1)}, bf16[64,7168]{1,0:T(8,128)(2,1)S(1)}, u32[]{:S(2)}, u32[]{:S(2)}) collective-permute-start(bf16[64,7168]{1,0:T(8,128)(2,1)} %get-tuple-element.60), channel_id=1, source_target_pairs={{0,16},{1,17},{2,18},{3,19},{4,20},{5,21},{6,22},{7,23},{8,24},{9,... | collective-permute-start | bytes 2752520 | tf_op jit(solution)/shard_map/ppermute | solution.py:43
  127.5 21.9 %collective-permute-start.23 = (bf16[64,7168]{1,0:T(8,128)(2,1)}, bf16[64,7168]{1,0:T(8,128)(2,1)S(1)}, u32[]{:S(2)}, u32[]{:S(2)}) collective-permute-start(bf16[64,7168]{1,0:T(8,128)(2,1)} %get-tuple-element.61), channel_id=1, source_target_pairs={{0,1},{1,2},{2,3},{3,0},{4,5},{5,6},{6,7},{7,4},{8,9},{9,10},{10,1... | collective-permute-start | bytes 2752520 | tf_op jit(solution)/shard_map/ppermute | solution.py:43
  128.9 20.5 %collective-permute-start.24 = (bf16[64,7168]{1,0:T(8,128)(2,1)}, bf16[64,7168]{1,0:T(8,128)(2,1)S(1)}, u32[]{:S(2)}, u32[]{:S(2)}) collective-permute-start(bf16[64,7168]{1,0:T(8,128)(2,1)} %get-tuple-element.63), channel_id=1, source_target_pairs={{0,3},{1,0},{2,1},{3,2},{4,7},{5,4},{6,5},{7,6},{8,11},{9,8},{10,9... | collective-permute-start | bytes 2752520 | tf_op jit(solution)/shard_map/ppermute | solution.py:43
  154.0 21.4 %collective-permute-start.33 = (bf16[80,7168]{1,0:T(8,128)(2,1)}, bf16[80,7168]{1,0:T(8,128)(2,1)S(1)}, u32[]{:S(2)}, u32[]{:S(2)}) collective-permute-start(bf16[80,7168]{1,0:T(8,128)(2,1)} %get-tuple-element.74), channel_id=1, source_target_pairs={{0,4},{1,5},{2,6},{3,7},{4,8},{5,9},{6,10},{7,11},{8,12},{9,13},{1... | collective-permute-start | bytes 3440648 | tf_op jit(solution)/shard_map/ppermute | solution.py:43
  156.2 13.4 %collective-permute-start.28 = (bf16[64,7168]{1,0:T(8,128)(2,1)}, bf16[64,7168]{1,0:T(8,128)(2,1)S(1)}, u32[]{:S(2)}, u32[]{:S(2)}) collective-permute-start(bf16[64,7168]{1,0:T(8,128)(2,1)} %get-tuple-element.70), channel_id=1, source_target_pairs={{0,16},{1,17},{2,18},{3,19},{4,20},{5,21},{6,22},{7,23},{8,24},{9,... | collective-permute-start | bytes 2752520 | tf_op jit(solution)/shard_map/ppermute | solution.py:43
  179.7 25.5 %collective-permute-start.34 = (bf16[80,7168]{1,0:T(8,128)(2,1)}, bf16[80,7168]{1,0:T(8,128)(2,1)S(1)}, u32[]{:S(2)}, u32[]{:S(2)}) collective-permute-start(bf16[80,7168]{1,0:T(8,128)(2,1)} %shard_map.110), channel_id=1, source_target_pairs={{0,4},{1,5},{2,6},{3,7},{4,8},{5,9},{6,10},{7,11},{8,12},{9,13},{1... | collective-permute-start | bytes 3440648 | tf_op jit(solution)/shard_map/ppermute | solution.py:43
  181.0 31.1 %collective-permute-start.39 = (bf16[80,7168]{1,0:T(8,128)(2,1)}, bf16[80,7168]{1,0:T(8,128)(2,1)}, u32[]{:S(2)}, u32[]{:S(2)}) collective-permute-start(bf16[80,7168]{1,0:T(8,128)(2,1)} %get-tuple-element.76), channel_id=1, source_target_pairs={{0,12},{1,13},{2,14},{3,15},{4,0},{5,1},{6,2},{7,3},{8,4},{9,5},{1... | collective-permute-start | bytes 3440648 | tf_op jit(solution)/shard_map/ppermute | solution.py:43
  181.2 22.7 %collective-permute-start.32 = (bf16[64,7168]{1,0:T(8,128)(2,1)S(1)}, bf16[64,7168]{1,0:T(8,128)(2,1)}, u32[]{:S(2)}, u32[]{:S(2)}) collective-permute-start(bf16[64,7168]{1,0:T(8,128)(2,1)S(1)} %copy-done.13), channel_id=1, source_target_pairs={{0,64},{1,65},{2,66},{3,67},{4,68},{5,69},{6,70},{7,71},{8,72},{9,... | collective-permute-start | bytes 2752520 | tf_op jit(solution)/shard_map/ppermute | solution.py:43
  190.0 13.2 %collective-permute-start.38 = (f32[1,7168]{1,0:T(1,128)S(1)}, f32[1,7168]{1,0:T(1,128)S(1)}, u32[]{:S(2)}, u32[]{:S(2)}) collective-permute-start(f32[1,7168]{1,0:T(1,128)S(1)} %add.320), channel_id=1, source_target_pairs={{0,64},{1,65},{2,66},{3,67},{4,68},{5,69},{6,70},{7,71},{8,72},{9,... | collective-permute-start | bytes 86024 | tf_op jit(solution)/shard_map/ppermute | solution.py:43
  (45 other events, 282.1 us)

commit v2 on v1

--- a/solution.py
+++ b/solution.py
@@ -9,7 +9,7 @@
 STEP = 100
 AXES = ("xh", "core", "xl", "z", "y")
 SIZES = (2, 2, 2, 4, 4)
-VMEM_LIMIT = 56 * 1024 * 1024
+MIB = 1024 * 1024
 BLOCK = 1792
 LANES = 128
 half = jnp.bfloat16
@@ -93,8 +93,8 @@
     return [pl.BlockSpec(memory_space=pl.ANY) for _ in arrays]
 
 
-def params():
-    return pltpu.CompilerParams(vmem_limit_bytes=VMEM_LIMIT)
+def params(mib):
+    return pltpu.CompilerParams(vmem_limit_bytes=mib * MIB)
 
 
 def cost(rows, columns, depth):
@@ -127,7 +127,7 @@
         out_shape=[jax.ShapeDtypeStruct((rows, width), dtype) for rows, dtype in outs]
         + [jax.ShapeDtypeStruct(array.shape, array.dtype) for array in passed],
         input_output_aliases={len(operands) + len(after) + i: len(outs) + i for i in range(len(passed))},
-        compiler_params=params(),
+        compiler_params=params(28),
         cost_estimate=pl.CostEstimate(flops=0, bytes_accessed=2 * size * width, transcendentals=0),
     )(*[array for array, _, _ in operands], *after, *passed)
 
@@ -160,7 +160,7 @@
             out_specs=pl.BlockSpec((block, width + LANES), lambda i, core_ref: (i, 0)),
         ),
         out_shape=jax.ShapeDtypeStruct((rows // 2, width + LANES), half),
-        compiler_params=params(),
+        compiler_params=params(28),
         cost_estimate=pl.CostEstimate(flops=0, bytes_accessed=16 * rows * width, transcendentals=0),
     )(core.reshape(1), hidden, gain.reshape(1, width), digits)
 
@@ -208,7 +208,7 @@
             jax.ShapeDtypeStruct((rows, columns), jnp.float32),
             jax.ShapeDtypeStruct((3, columns), jnp.float32),
         ],
-        compiler_params=params(),
+        compiler_params=params(28),
         cost_estimate=cost(rows, columns, width),
     )(*head, *tokens, *tokens, *after)
 
@@ -236,7 +236,7 @@
 
 
 def token_grads(near, flip, stats, wanted, head):
-    rows, columns = near.shape[0], near.shape[1] * 2
+    rows, columns = near.shape[0], near.shape[1] + flip.shape[1]
     width, part = head[0].shape[1], columns // 8
     return pl.pallas_call(
         lambda *refs: token_grad_kernel(len(head), part, *refs),
@@ -245,7 +245,7 @@
         out_specs=[whole((rows, columns))] + [pl.BlockSpec((part, BLOCK), lambda i: (0, i))] * 8,
         out_shape=[jax.ShapeDtypeStruct((rows, columns), half)] + [jax.ShapeDtypeStruct((part, width), half)] * 8,
         scratch_shapes=[pltpu.VMEM((columns, rows), half)],
-        compiler_params=params(),
+        compiler_params=params(56),
         cost_estimate=cost(rows, columns, width),
     )(near, flip, stats, wanted, *head)
 
@@ -273,7 +273,7 @@
             jax.ShapeDtypeStruct((rows // 2, width), half),
             jax.ShapeDtypeStruct((1, width), jnp.float32),
         ],
-        compiler_params=params(),
+        compiler_params=params(28),
         cost_estimate=cost(rows, columns, width),
     )(grads, *head, *tokens)
 
@@ -283,7 +283,9 @@
     scale = lax.rsqrt(jnp.mean(hfloat * hfloat, axis=-1, keepdims=True) + 1e-06)
     scaled = (wide(mine_ref[...]) + wide(their_ref[...])) * gain_ref[...]
     dot_mean = jnp.mean(scaled * hfloat, axis=-1, keepdims=True)
-    refs[-1][...] = short(scale * scaled - hfloat * scale**3 * dot_mean)
+    grads = short(scale * scaled - hfloat * scale**3 * dot_mean)
+    for ref in refs[-2:]:
+        ref[...] = grads
 
 
 def hidden_grads(mine, their, hidden, gain, core, after):
@@ -301,10 +303,13 @@
                 pl.BlockSpec((1, width), lambda i, core_ref: (0, 0)),
             ]
             + anywhere(after),
-            out_specs=pl.BlockSpec((block, width), lambda i, core_ref: (i, 0)),
+            out_specs=[
+                pl.BlockSpec((block, width), lambda i, core_ref: (i, 0)),
+                pl.BlockSpec((block, width), lambda i, core_ref: (core_ref[0] * 2 + i, 0)),
+            ],
         ),
-        out_shape=jax.ShapeDtypeStruct((rows // 2, width), half),
-        compiler_params=params(),
+        out_shape=[jax.ShapeDtypeStruct((size, width), half) for size in (rows // 2, rows)],
+        compiler_params=params(28),
         cost_estimate=pl.CostEstimate(flops=0, bytes_accessed=4 * rows * width, transcendentals=0),
     )(core.reshape(1), mine, their, hidden, gain.reshape(1, width), *after)
 
@@ -333,12 +338,12 @@
     other_far = along_core(head_far)
 
     head = [head_weight, head_after, head_far, head_before, other_own, other_after, other_far, other_before]
-    near_tokens = [own, own_after, own_far, own_before]
-    flip_tokens = [flip_own, flip_after, flip_far, flip_before]
+    near_tokens = [own, own_after, own_far, own_before, flip_own, flip_after]
+    flip_tokens = [flip_far, flip_before]
     near_logits, near_stats = all_logits(head, near_tokens)
     flip_logits, flip_stats = all_logits(head, flip_tokens, after=[near_stats])
 
-    stats = jnp.stack([near_stats[:2], flip_stats[:2]], axis=1).reshape(2, 2, 4, part)
+    stats = jnp.concatenate([near_stats[:2], flip_stats[:2]], axis=1).reshape(2, 2, 4, part)
     stats = merge(jnp.stack([stats] + [jnp.roll(along_y(stats, by), -by, axis=2) for by in (1, 2, 3)]))
     stats = merge(jnp.stack([stats] + [jnp.roll(along_x(stats, by), by, axis=1) for by in (1, 2, 3)]))
     stats = stats.reshape(2, 8 * part)
@@ -372,7 +377,8 @@
     other_head = along_core(other_head)
     sum_before = along_y(sum_before, -1)
     gain_sum = gain_sum + move(gain_sum, lambda x, core, z, y: (x, core, z ^ 1, y))
-    gain_other = move(gain_sum, lambda x, core, z, y: (x, core, z + 2, y))
+    gain_sum = gain_sum + move(gain_sum, lambda x, core, z, y: (x, core, z + 2, y))
+    gain_other = along_core(gain_sum)
     head_far, head_before, gain_sum = by_strips(
         lambda mine, theirs, mine_too, theirs_too, g_sum, g_other: (
             mine + wide(theirs),
@@ -384,39 +390,37 @@
         + all_rows(gain_sum, gain_other),
         [(held, half), (held, half), (1, jnp.float32)],
     )
-
-    sum_after, flip_own, head_far, head_before, gain_sum = by_strips(
+    head_far = along_z(head_far, 1)
+
+    sum_after, flip_own, gain_sum = by_strips(
         lambda after, f_after, far, own, before: (wide(after) + wide(f_after) + wide(far), wide(own) + wide(before)),
         all_rows(sum_after, flip_after, sum_far, flip_own, flip_before),
         [(part, half), (part, half)],
         after=[sum_before],
-        passed=[head_far, head_before, gain_sum],
+        passed=[gain_sum],
     )
     sum_after = along_y(sum_after, 1)
     flip_own = flip_x(flip_own)
-    head_far, head_before = along_z(head_far, 1), along_z(head_before, -1)
-    gain_sum = gain_sum + along_core(gain_sum)
     gain_other = move(gain_sum, lambda x, core, z, y: (x ^ 1, core, z, y))
 
-    summed, gain_sum = by_strips(
-        lambda a, b, c, d, mine, theirs: (wide(a) + wide(b) + (wide(c) + wide(d)), mine + theirs),
-        all_rows(sum_own, flip_own, sum_after, sum_before, gain_sum, gain_other),
-        [(part, half), (1, jnp.float32)],
-    )
-    (head_after,) = by_strips(
-        lambda mine, theirs, far: (mine + wide(theirs) + wide(far),),
-        [(near_head, held, held), (other_head, held, held), (head_far, 0, held)],
-        [(held, half)],
-        after=[summed],
-    )
-    head_after = along_z(head_after, 1)
-    grad_hidden = hidden_grads(summed, along_x(summed, 2), hidden, gain, core, [head_after])
+    head_after, gain_sum, head_before = by_strips(
+        lambda mine, theirs, far, g_sum, g_other: (mine + wide(theirs) + wide(far), g_sum + g_other),
+        [(near_head, held, held), (other_head, held, held)] + all_rows(head_far, gain_sum, gain_other),
+        [(held, half), (1, jnp.float32)],
+        after=[sum_after],
+        passed=[head_before],
+    )
+
+    (summed,) = by_strips(
+        lambda a, b, c, d: (wide(a) + wide(b) + (wide(c) + wide(d)),),
+        all_rows(sum_own, flip_own, sum_after, sum_before),
+        [(part, half)],
+        after=[head_after],
+    )
+    head_after, head_before = along_z(head_after, 1), along_z(head_before, -1)
+    grad_hidden, placed = hidden_grads(summed, along_x(summed, 2), hidden, gain, core, [])
     other_half = along_core(grad_hidden)
-    grad_hidden = jnp.where(
-        core == 0,
-        jnp.concatenate([grad_hidden, other_half]),
-        jnp.concatenate([other_half, grad_hidden]),
-    )
+    grad_hidden = lax.dynamic_update_slice(placed, other_half, ((1 - core) * part, 0))
 
     gain_sum = gain_sum + move(gain_sum, lambda x, core, z, y: (x, core, z, y ^ 1))
     gain_sum = gain_sum + move(gain_sum, lambda x, core, z, y: (x, core, z, y + 2))

time: 220 us -> 202 us (0.918)
  Pallas kernels: 61.5 us -> 45.9 us
  starting transfers between devices: 63.2 us -> 57.7 us
  waiting for transfers between devices: 68 us -> 72.2 us
  other arithmetic: 11.9 us -> 8.59 us
    pallas_call x5, Pallas kernels: 16.3 us -> 6.3 us  [by_strips(): pl.pallas_call(kernel, grid=(width // block,), in_specs=[strip(rows, star...]
    ppermute x40, starting transfers between devices: 63.2 us -> 57.7 us  [move(): return lax.ppermute(array, AXES, pairs)]
    unnamed x59 -> x68, local copies, waits for them, and re-layouts: 10.2 us -> 15 us
    ppermute x40, waiting for transfers between devices: 68 us -> 72.2 us  [move(): return lax.ppermute(array, AXES, pairs)]
    pallas_call x1, Pallas kernels: 12.8 us -> 10.1 us  [head_grads(): pl.pallas_call(lambda *refs: head_grad_kernel(len(head), len(tokens), *re...]
  transfers between devices with their start and end apart: 40 -> 40, of which waited for: 20 -> 22; matrix products, arithmetic and copies ran while one was open for 5% -> 4% of each run, Pallas kernels for 15% -> 14%
where the time goes in v2:
time: 202 us; the launch traced here: 201 us
  waiting for transfers between devices  72.2 us (36%)
  starting transfers between devices  57.7 us (29%)
  Pallas kernels  45.9 us (23%)
  local copies, waits for them, and re-layouts  15.4 us (8%)
  other arithmetic  8.59 us (4%)
    ppermute x40, waiting for transfers between devices, move(): return lax.ppermute(array, AXES, pairs)  72.2 us
    ppermute x40, starting transfers between devices, move(): return lax.ppermute(array, AXES, pairs)  57.7 us
    unnamed x68, local copies, waits for them, and re-layouts  15 us
    pallas_call x2, Pallas kernels, all_logits(): pl.pallas_call(lambda *refs: logits_kernel(len(head), len(tokens), *refs)...  14.3 us
    pallas_call x1, Pallas kernels, token_grads(): pl.pallas_call(lambda *refs: token_grad_kernel(len(head), part, *refs), g...  11.5 us
    pallas_call x1, Pallas kernels, head_grads(): pl.pallas_call(lambda *refs: head_grad_kernel(len(head), len(tokens), *re...  10.1 us
    pallas_call x5, Pallas kernels, by_strips(): pl.pallas_call(kernel, grid=(width // block,), in_specs=[strip(rows, star...  6.3 us
    convert_element_type x1, other arithmetic, adam_step(): (wfloat - 0.001 * update).astype(jnp.bfloat16)  5.65 us
  transfers between devices with their start and end apart: 40, of which 22 were waited for; matrix products, arithmetic and copies ran while one was open for 4% of the time, Pallas kernels for 14%

profile of v2, /device:TPU:1, one launch (start us, length us, event | category | flops | bytes accessed | tf_op | source)
XLA Modules:
  0.0 201.0 jit_solution(5187788156519678727)
XLA Ops:
  0.6 2.5 %collective-permute-start = (bf16[80,7168]{1,0:T(8,128)(2,1)}, bf16[80,7168]{1,0:T(8,128)(2,1)S(1)}, u32[]{:S(2)}, u32[]{:S(2)}) collective-permute-start(bf16[80,7168]{1,0:T(8,128)(2,1)} %refs_1_.1), channel_id=1, source_target_pairs={{0,12},{1,13},{2,14},{3,15},{4,0},{5,1},{6,2},{7,3},{8,4},{9,5},{1... | collective-permute-start | bytes 3440648 | tf_op jit(solution)/shard_map/ppermute | solution.py:43
  14.4 4.9 %collective-permute-done.refs_1_.refs_5_.refs_2_ = bf16[80,7168]{1,0:T(8,128)(2,1)S(1)} collective-permute-done((bf16[80,7168]{1,0:T(8,128)(2,1)}, bf16[80,7168]{1,0:T(8,128)(2,1)S(1)}, u32[]{:S(2)}, u32[]{:S(2)}) %collective-permute-start) | collective-permute-done | bytes 1146912 | tf_op jit(solution)/shard_map/ppermute | solution.py:43
  20.8 3.6 %collective-permute-done.7.refs_9_.refs_15_.refs_10_ = bf16[64,7296]{1,0:T(8,128)(2,1)S(1)} collective-permute-done((bf16[64,7296]{1,0:T(8,128)(2,1)S(1)}, bf16[64,7296]{1,0:T(8,128)(2,1)S(1)}, u32[]{:S(2)}, u32[]{:S(2)}) %collective-permute-start.7) | collective-permute-done | bytes 933920 | tf_op jit(solution)/shard_map/ppermute | solution.py:43
  24.4 4.3 %collective-permute-done.8.refs_11_.refs_17_.refs_12_ = bf16[64,7296]{1,0:T(8,128)(2,1)S(1)} collective-permute-done((bf16[64,7296]{1,0:T(8,128)(2,1)S(1)}, bf16[64,7296]{1,0:T(8,128)(2,1)S(1)}, u32[]{:S(2)}, u32[]{:S(2)}) %collective-permute-start.8) | collective-permute-done | bytes 933920 | tf_op jit(solution)/shard_map/ppermute | solution.py:43
  30.9 4.3 %collective-permute-start.3 = (bf16[80,7168]{1,0:T(8,128)(2,1)S(1)}, bf16[80,7168]{1,0:T(8,128)(2,1)S(1)}, u32[]{:S(2)}, u32[]{:S(2)}) collective-permute-start(bf16[80,7168]{1,0:T(8,128)(2,1)S(1)} %copy-done.2), channel_id=1, source_target_pairs={{0,32},{1,33},{2,34},{3,35},{4,36},{5,37},{6,38},{7,39},{8,40},{9,... | collective-permute-start | bytes 3440648 | tf_op jit(solution)/shard_map/ppermute | solution.py:43
  35.3 2.5 %collective-permute-start.11 = (bf16[64,7296]{1,0:T(8,128)(2,1)S(1)}, bf16[64,7296]{1,0:T(8,128)(2,1)S(1)}, u32[]{:S(2)}, u32[]{:S(2)}) collective-permute-start(bf16[64,7296]{1,0:T(8,128)(2,1)S(1)} %collective-permute-done.7.refs_9_.refs_15_.refs_10_), channel_id=1, source_target_pairs={{0,16},{1,17},{2,18},{3,19},{4,20},{5,21},{6,22},{7,23},{8,24},{9,... | collective-permute-start | bytes 2801672 | tf_op jit(solution)/shard_map/ppermute | solution.py:43
  38.7 4.9 %collective-permute-done.10.refs_10_.refs_16_.refs_11_ = bf16[64,7296]{1,0:T(8,128)(2,1)} collective-permute-done((bf16[64,7296]{1,0:T(8,128)(2,1)S(1)}, bf16[64,7296]{1,0:T(8,128)(2,1)}, u32[]{:S(2)}, u32[]{:S(2)}) %collective-permute-start.10) | collective-permute-done | bytes 933920 | tf_op jit(solution)/shard_map/ppermute | solution.py:43
  43.6 2.8 %collective-permute-start.6 = (bf16[80,7168]{1,0:T(8,128)(2,1)}, bf16[80,7168]{1,0:T(8,128)(2,1)}, u32[]{:S(2)}, u32[]{:S(2)}) collective-permute-start(bf16[80,7168]{1,0:T(8,128)(2,1)} %collective-permute-done.2.refs_3_.refs_7_.refs_4_), channel_id=1, source_target_pairs={{0,32},{1,33},{2,34},{3,35},{4,36},{5,37},{6,38},{7,39},{8,40},{9,... | collective-permute-start | bytes 3440648 | tf_op jit(solution)/shard_map/ppermute | solution.py:43
  59.2 8.5 %shard_map.102 = (f32[640,384]{1,0:T(8,128)S(1)}, f32[3,384]{1,0:T(4,128)S(1)}) custom-call(bf16[80,7168]{1,0:T(8,128)(2,1)S(1)} %copy-done.2, bf16[80,7168]{1,0:T(8,128)(2,1)S(1)} %collective-permute-done.refs_1_.refs_5_.refs_2_, bf16[80,7168]{1,0:T(8,128)(2,1)} %collective-permute-done.1.refs_2_.refs_6_.refs_3_, ...), custom_call_target="tpu_custom_call" | custom-call | flops 3523215360 | bytes 14680064 | tf_op jit(solution)/shard_map/pallas_call | solution.py:202
  68.6 5.8 %shard_map.103 = (f32[640,128]{1,0:T(8,128)S(1)}, f32[3,128]{1,0:T(4,128)S(1)}) custom-call(bf16[80,7168]{1,0:T(8,128)(2,1)S(1)} %copy-done.2, bf16[80,7168]{1,0:T(8,128)(2,1)S(1)} %collective-permute-done.refs_1_.refs_5_.refs_2_, bf16[80,7168]{1,0:T(8,128)(2,1)} %collective-permute-done.1.refs_2_.refs_6_.refs_3_, ...), custom_call_target="tpu_custom_call" | custom-call | flops 1174405120 | bytes 11010048 | tf_op jit(solution)/shard_map/pallas_call | solution.py:202
  82.2 2.7 %collective-permute-start.19 = (f32[2,2,4,64]{3,2,1,0:T(4,128)S(1)}, f32[2,2,4,64]{3,2,1,0:T(4,128)S(1)}, u32[]{:S(2)}, u32[]{:S(2)}) collective-permute-start(f32[2,2,4,64]{3,2,1,0:T(4,128)S(1)} %get-tuple-element.83), channel_id=1, source_target_pairs={{0,80},{1,81},{2,82},{3,83},{4,84},{5,85},{6,86},{7,87},{8,88},{9,... | collective-permute-start | bytes 12296 | tf_op jit(solution)/shard_map/ppermute | solution.py:43
  85.6 3.2 %collective-permute-done.18 = f32[2,2,4,64]{3,2,1,0:T(4,128)S(1)} collective-permute-done((f32[2,2,4,64]{3,2,1,0:T(4,128)S(1)}, f32[2,2,4,64]{3,2,1,0:T(4,128)S(1)}, u32[]{:S(2)}, u32[]{:S(2)}) %collective-permute-start.18) | collective-permute-done | bytes 4128 | tf_op jit(solution)/shard_map/ppermute | solution.py:43
  89.7 11.5 %shard_map.104 = (bf16[640,512]{1,0:T(8,128)(2,1)}, bf16[64,7168]{1,0:T(8,128)(2,1)}, bf16[64,7168]{1,0:T(8,128)(2,1)}, bf16[64,7168]{1,0:T(8,128)(2,1)}, bf16[6...) custom-call(f32[640,384]{1,0:T(8,128)} %copy-done.28, ...), custom_call_target="tpu_custom_call" | custom-call | flops 4697620480 | bytes 16515072 | tf_op jit(solution)/shard_map/pallas_call | solution.py:241
  102.5 10.1 %shard_map.105 = (f32[320,7168]{1,0:T(8,128)}, bf16[320,7168]{1,0:T(8,128)(2,1)S(1)}, f32[1,7168]{1,0:T(1,128)S(1)}) custom-call(bf16[640,512]{1,0:T(8,128)(2,1)S(1)} %copy-done.30, bf16[80,7168]{1,0:T(8,128)(2,1)S(1)} %copy-done.3, bf16[80,7168]{1,0:T(8,128)(2,1)S(1)} %copy-done.7, bf16[80,7168]{1,0:T(8,128)(2,1)} %collective-permute-done.1.refs_2_.refs_6_.refs_3_, ...), custom_call_target="tpu_custom_call" | custom-call | flops 4697620480 | bytes 16515072 | tf_op jit(solution)/shard_map/pallas_call | solution.py:266
  115.8 3.4 %collective-permute-start.25 = (bf16[320,7168]{1,0:T(8,128)(2,1)S(1)}, bf16[320,7168]{1,0:T(8,128)(2,1)S(1)}, u32[]{:S(2)}, u32[]{:S(2)}) collective-permute-start(bf16[320,7168]{1,0:T(8,128)(2,1)S(1)} %get-tuple-element.66), channel_id=1, source_target_pairs={{0,32},{1,33},{2,34},{3,35},{4,36},{5,37},{6,38},{7,39},{8,40},{9,... | collective-permute-start | bytes 13762568 | tf_op jit(solution)/shard_map/ppermute | solution.py:43
  120.9 3.2 %collective-permute-start.23 = (bf16[64,7168]{1,0:T(8,128)(2,1)S(1)}, bf16[64,7168]{1,0:T(8,128)(2,1)S(1)}, u32[]{:S(2)}, u32[]{:S(2)}) collective-permute-start(bf16[64,7168]{1,0:T(8,128)(2,1)S(1)} %get-tuple-element.62), channel_id=1, source_target_pairs={{0,1},{1,2},{2,3},{3,0},{4,5},{5,6},{6,7},{7,4},{8,9},{9,10},{10,1... | collective-permute-start | bytes 2752520 | tf_op jit(solution)/shard_map/ppermute | solution.py:43
  127.2 2.9 %collective-permute-start.27 = (f32[1,7168]{1,0:T(1,128)S(1)}, f32[1,7168]{1,0:T(1,128)S(1)}, u32[]{:S(2)}, u32[]{:S(2)}) collective-permute-start(f32[1,7168]{1,0:T(1,128)S(1)} %add.320), channel_id=1, source_target_pairs={{0,8},{1,9},{2,10},{3,11},{4,12},{5,13},{6,14},{7,15},{8,0},{9,1},... | collective-permute-start | bytes 86024 | tf_op jit(solution)/shard_map/ppermute | solution.py:43
  137.1 5.9 %collective-permute-done.23.refs_2_ = bf16[64,7168]{1,0:T(8,128)(2,1)S(1)} collective-permute-done((bf16[64,7168]{1,0:T(8,128)(2,1)S(1)}, bf16[64,7168]{1,0:T(8,128)(2,1)S(1)}, u32[]{:S(2)}, u32[]{:S(2)}) %collective-permute-start.23) | collective-permute-done | bytes 917536 | tf_op jit(solution)/shard_map/ppermute | solution.py:43
  144.5 3.0 %collective-permute-start.30 = (bf16[64,7168]{1,0:T(8,128)(2,1)S(1)}, bf16[64,7168]{1,0:T(8,128)(2,1)S(1)}, u32[]{:S(2)}, u32[]{:S(2)}) collective-permute-start(bf16[64,7168]{1,0:T(8,128)(2,1)S(1)} %get-tuple-element.70), channel_id=1, source_target_pairs={{0,1},{1,2},{2,3},{3,0},{4,5},{5,6},{6,7},{7,4},{8,9},{9,10},{10,1... | collective-permute-start | bytes 2752520 | tf_op jit(solution)/shard_map/ppermute | solution.py:43
  149.0 11.1 %collective-permute-done.32.refs_4_ = f32[1,7168]{1,0:T(1,128)S(1)} collective-permute-done((f32[1,7168]{1,0:T(1,128)S(1)}, f32[1,7168]{1,0:T(1,128)S(1)}, u32[]{:S(2)}, u32[]{:S(2)}) %collective-permute-start.32) | collective-permute-done | bytes 28704 | tf_op jit(solution)/shard_map/ppermute | solution.py:43
  169.6 4.1 %collective-permute-done.36 = f32[1,7168]{1,0:T(1,128)S(1)} collective-permute-done((f32[1,7168]{1,0:T(1,128)S(1)}, f32[1,7168]{1,0:T(1,128)S(1)}, u32[]{:S(2)}, u32[]{:S(2)}) %collective-permute-start.36) | collective-permute-done | bytes 28704 | tf_op jit(solution)/shard_map/ppermute | solution.py:43
  175.7 13.7 %collective-permute-done.37 = f32[1,7168]{1,0:T(1,128)S(1)} collective-permute-done((f32[1,7168]{1,0:T(1,128)S(1)}, f32[1,7168]{1,0:T(1,128)S(1)}, u32[]{:S(2)}, u32[]{:S(2)}) %collective-permute-start.37) | collective-permute-done | bytes 28704 | tf_op jit(solution)/shard_map/ppermute | solution.py:43
  190.1 3.1 %shard_map.111 = (bf16[64,7168]{1,0:T(8,128)(2,1)S(1)}, bf16[128,7168]{1,0:T(8,128)(2,1)}) custom-call(s32[1]{0:T(128)} %bitcast.core_ref, bf16[64,7168]{1,0:T(8,128)(2,1)} %shard_map.110.mine_ref, bf16[64,7168]{1,0:T(8,128)(2,1)} %collective-permute-done.33.their_ref, bf16[128,7168]{1,0:T(8,128)(2,1)S(1)} %copy-done.5, f32[1,7168]{1,0:T(1,128)S(1)} %bitcast.50), custom_call_target="tpu_custom_call" | custom-call | bytes 3670016 | tf_op jit(solution)/shard_map/pallas_call | solution.py:294
  194.1 5.6 %fusion.2 = (bf16[80,7168]{1,0:T(8,128)(2,1)}, f32[80,7168]{1,0:T(8,128)}, f32[80,7168]{1,0:T(8,128)}) fusion(bf16[80,7168]{1,0:T(8,128)(2,1)S(1)} %copy-done.3, bf16[80,7168]{1,0:T(8,128)(2,1)} %collective-permute-done.39, bf16[80,7168]{1,0:T(8,128)(2,1)} %collective-permute-done.38, bf16[320,7168]{1,0:T(8,128)(2,1)} %copy-done.1, ...), kind=kLoop, calls=%fused_computation.5 | loop fusion | flops 13189120 | bytes 17203200 | tf_op jit(solution)/shard_map/convert_element_type | solution.py:25
  (175 shorter events, 72.2 us)
Async XLA Ops:
  0.6 18.7 %collective-permute-start = (bf16[80,7168]{1,0:T(8,128)(2,1)}, bf16[80,7168]{1,0:T(8,128)(2,1)S(1)}, u32[]{:S(2)}, u32[]{:S(2)}) collective-permute-start(bf16[80,7168]{1,0:T(8,128)(2,1)} %refs_1_.1), channel_id=1, source_target_pairs={{0,12},{1,13},{2,14},{3,15},{4,0},{5,1},{6,2},{7,3},{8,4},{9,5},{1... | collective-permute-start | bytes 3440648 | tf_op jit(solution)/shard_map/ppermute | solution.py:43
  6.8 17.6 %collective-permute-start.7 = (bf16[64,7296]{1,0:T(8,128)(2,1)S(1)}, bf16[64,7296]{1,0:T(8,128)(2,1)S(1)}, u32[]{:S(2)}, u32[]{:S(2)}) collective-permute-start(bf16[64,7296]{1,0:T(8,128)(2,1)S(1)} %shard_map.101.refs_8_.refs_14_.refs_9_), channel_id=1, source_target_pairs={{0,3},{1,0},{2,1},{3,2},{4,7},{5,4},{6,5},{7,6},{8,11},{9,8},{10,9... | collective-permute-start | bytes 2801672 | tf_op jit(solution)/shard_map/ppermute | solution.py:43
  8.2 20.5 %collective-permute-start.8 = (bf16[64,7296]{1,0:T(8,128)(2,1)S(1)}, bf16[64,7296]{1,0:T(8,128)(2,1)S(1)}, u32[]{:S(2)}, u32[]{:S(2)}) collective-permute-start(bf16[64,7296]{1,0:T(8,128)(2,1)S(1)} %shard_map.101.refs_8_.refs_14_.refs_9_), channel_id=1, source_target_pairs={{0,1},{1,2},{2,3},{3,0},{4,5},{5,6},{6,7},{7,4},{8,9},{9,10},{10,1... | collective-permute-start | bytes 2801672 | tf_op jit(solution)/shard_map/ppermute | solution.py:43
  9.7 20.0 %collective-permute-start.9 = (bf16[64,7296]{1,0:T(8,128)(2,1)S(1)}, bf16[64,7296]{1,0:T(8,128)(2,1)}, u32[]{:S(2)}, u32[]{:S(2)}) collective-permute-start(bf16[64,7296]{1,0:T(8,128)(2,1)S(1)} %shard_map.101.refs_8_.refs_14_.refs_9_), channel_id=1, source_target_pairs={{0,16},{1,17},{2,18},{3,19},{4,20},{5,21},{6,22},{7,23},{8,24},{9,... | collective-permute-start | bytes 2801672 | tf_op jit(solution)/shard_map/ppermute | solution.py:43
  12.2 26.6 %collective-permute-start.2 = (bf16[80,7168]{1,0:T(8,128)(2,1)S(1)}, bf16[80,7168]{1,0:T(8,128)(2,1)}, u32[]{:S(2)}, u32[]{:S(2)}) collective-permute-start(bf16[80,7168]{1,0:T(8,128)(2,1)S(1)} %copy-done.2), channel_id=1, source_target_pairs={{0,4},{1,5},{2,6},{3,7},{4,8},{5,9},{6,10},{7,11},{8,12},{9,13},{1... | collective-permute-start | bytes 3440648 | tf_op jit(solution)/shard_map/ppermute | solution.py:43
  19.3 27.0 %collective-permute-start.1 = (bf16[80,7168]{1,0:T(8,128)(2,1)S(1)}, bf16[80,7168]{1,0:T(8,128)(2,1)}, u32[]{:S(2)}, u32[]{:S(2)}) collective-permute-start(bf16[80,7168]{1,0:T(8,128)(2,1)S(1)} %collective-permute-done.refs_1_.refs_5_.refs_2_), channel_id=1, source_target_pairs={{0,12},{1,13},{2,14},{3,15},{4,0},{5,1},{6,2},{7,3},{8,4},{9,5},{1... | collective-permute-start | bytes 3440648 | tf_op jit(solution)/shard_map/ppermute | solution.py:43
  29.7 13.9 %collective-permute-start.10 = (bf16[64,7296]{1,0:T(8,128)(2,1)S(1)}, bf16[64,7296]{1,0:T(8,128)(2,1)}, u32[]{:S(2)}, u32[]{:S(2)}) collective-permute-start(bf16[64,7296]{1,0:T(8,128)(2,1)S(1)} %collective-permute-done.7.refs_9_.refs_15_.refs_10_), channel_id=1, source_target_pairs={{0,3},{1,0},{2,1},{3,2},{4,7},{5,4},{6,5},{7,6},{8,11},{9,8},{10,9... | collective-permute-start | bytes 2801672 | tf_op jit(solution)/shard_map/ppermute | solution.py:43
  30.9 19.9 %collective-permute-start.3 = (bf16[80,7168]{1,0:T(8,128)(2,1)S(1)}, bf16[80,7168]{1,0:T(8,128)(2,1)S(1)}, u32[]{:S(2)}, u32[]{:S(2)}) collective-permute-start(bf16[80,7168]{1,0:T(8,128)(2,1)S(1)} %copy-done.2), channel_id=1, source_target_pairs={{0,32},{1,33},{2,34},{3,35},{4,36},{5,37},{6,38},{7,39},{8,40},{9,... | collective-permute-start | bytes 3440648 | tf_op jit(solution)/shard_map/ppermute | solution.py:43
  35.3 13.0 %collective-permute-start.11 = (bf16[64,7296]{1,0:T(8,128)(2,1)S(1)}, bf16[64,7296]{1,0:T(8,128)(2,1)S(1)}, u32[]{:S(2)}, u32[]{:S(2)}) collective-permute-start(bf16[64,7296]{1,0:T(8,128)(2,1)S(1)} %collective-permute-done.7.refs_9_.refs_15_.refs_10_), channel_id=1, source_target_pairs={{0,16},{1,17},{2,18},{3,19},{4,20},{5,21},{6,22},{7,23},{8,24},{9,... | collective-permute-start | bytes 2801672 | tf_op jit(solution)/shard_map/ppermute | solution.py:43
  38.7 15.6 %collective-permute-start.4 = (bf16[80,7168]{1,0:T(8,128)(2,1)S(1)}, bf16[80,7168]{1,0:T(8,128)(2,1)}, u32[]{:S(2)}, u32[]{:S(2)}) collective-permute-start(bf16[80,7168]{1,0:T(8,128)(2,1)S(1)} %collective-permute-done.refs_1_.refs_5_.refs_2_), channel_id=1, source_target_pairs={{0,32},{1,33},{2,34},{3,35},{4,36},{5,37},{6,38},{7,39},{8,40},{9,... | collective-permute-start | bytes 3440648 | tf_op jit(solution)/shard_map/ppermute | solution.py:43
  49.2 19.4 %collective-permute-start.13 = (bf16[64,7296]{1,0:T(8,128)(2,1)}, bf16[64,7296]{1,0:T(8,128)(2,1)}, u32[]{:S(2)}, u32[]{:S(2)}) collective-permute-start(bf16[64,7296]{1,0:T(8,128)(2,1)} %collective-permute-done.9.refs_12_.refs_18_.refs_13_), channel_id=1, source_target_pairs={{0,1},{1,2},{2,3},{3,0},{4,5},{5,6},{6,7},{7,4},{8,9},{9,10},{10,1... | collective-permute-start | bytes 2801672 | tf_op jit(solution)/shard_map/ppermute | solution.py:43
  51.8 16.8 %collective-permute-start.12 = (bf16[64,7296]{1,0:T(8,128)(2,1)}, bf16[64,7296]{1,0:T(8,128)(2,1)}, u32[]{:S(2)}, u32[]{:S(2)}) collective-permute-start(bf16[64,7296]{1,0:T(8,128)(2,1)} %collective-permute-done.10.refs_10_.refs_16_.refs_11_), channel_id=1, source_target_pairs={{0,16},{1,17},{2,18},{3,19},{4,20},{5,21},{6,22},{7,23},{8,24},{9,... | collective-permute-start | bytes 2801672 | tf_op jit(solution)/shard_map/ppermute | solution.py:43
  101.3 14.0 %collective-permute-start.21 = (bf16[64,7168]{1,0:T(8,128)(2,1)}, bf16[64,7168]{1,0:T(8,128)(2,1)S(1)}, u32[]{:S(2)}, u32[]{:S(2)}) collective-permute-start(bf16[64,7168]{1,0:T(8,128)(2,1)} %get-tuple-element.57), channel_id=1, source_target_pairs={{0,3},{1,0},{2,1},{3,2},{4,7},{5,4},{6,5},{7,6},{8,11},{9,8},{10,9... | collective-permute-start | bytes 2752520 | tf_op jit(solution)/shard_map/ppermute | solution.py:43
  115.8 17.4 %collective-permute-start.25 = (bf16[320,7168]{1,0:T(8,128)(2,1)S(1)}, bf16[320,7168]{1,0:T(8,128)(2,1)S(1)}, u32[]{:S(2)}, u32[]{:S(2)}) collective-permute-start(bf16[320,7168]{1,0:T(8,128)(2,1)S(1)} %get-tuple-element.66), channel_id=1, source_target_pairs={{0,32},{1,33},{2,34},{3,35},{4,36},{5,37},{6,38},{7,39},{8,40},{9,... | collective-permute-start | bytes 13762568 | tf_op jit(solution)/shard_map/ppermute | solution.py:43
  119.2 17.9 %collective-permute-start.22 = (bf16[64,7168]{1,0:T(8,128)(2,1)S(1)}, bf16[64,7168]{1,0:T(8,128)(2,1)S(1)}, u32[]{:S(2)}, u32[]{:S(2)}) collective-permute-start(bf16[64,7168]{1,0:T(8,128)(2,1)S(1)} %get-tuple-element.61), channel_id=1, source_target_pairs={{0,16},{1,17},{2,18},{3,19},{4,20},{5,21},{6,22},{7,23},{8,24},{9,... | collective-permute-start | bytes 2752520 | tf_op jit(solution)/shard_map/ppermute | solution.py:43
  120.9 22.1 %collective-permute-start.23 = (bf16[64,7168]{1,0:T(8,128)(2,1)S(1)}, bf16[64,7168]{1,0:T(8,128)(2,1)S(1)}, u32[]{:S(2)}, u32[]{:S(2)}) collective-permute-start(bf16[64,7168]{1,0:T(8,128)(2,1)S(1)} %get-tuple-element.62), channel_id=1, source_target_pairs={{0,1},{1,2},{2,3},{3,0},{4,5},{5,6},{6,7},{7,4},{8,9},{9,10},{10,1... | collective-permute-start | bytes 2752520 | tf_op jit(solution)/shard_map/ppermute | solution.py:43
  124.1 19.4 %collective-permute-start.24 = (bf16[64,7168]{1,0:T(8,128)(2,1)S(1)}, bf16[64,7168]{1,0:T(8,128)(2,1)S(1)}, u32[]{:S(2)}, u32[]{:S(2)}) collective-permute-start(bf16[64,7168]{1,0:T(8,128)(2,1)S(1)} %get-tuple-element.64), channel_id=1, source_target_pairs={{0,3},{1,0},{2,1},{3,2},{4,7},{5,4},{6,5},{7,6},{8,11},{9,8},{10,9... | collective-permute-start | bytes 2752520 | tf_op jit(solution)/shard_map/ppermute | solution.py:43
  135.0 25.1 %collective-permute-start.31 = (bf16[80,7168]{1,0:T(8,128)(2,1)S(1)}, bf16[80,7168]{1,0:T(8,128)(2,1)S(1)}, u32[]{:S(2)}, u32[]{:S(2)}) collective-permute-start(bf16[80,7168]{1,0:T(8,128)(2,1)S(1)} %get-tuple-element.71), channel_id=1, source_target_pairs={{0,4},{1,5},{2,6},{3,7},{4,8},{5,9},{6,10},{7,11},{8,12},{9,13},{1... | collective-permute-start | bytes 3440648 | tf_op jit(solution)/shard_map/ppermute | solution.py:43
  144.5 15.6 %collective-permute-start.30 = (bf16[64,7168]{1,0:T(8,128)(2,1)S(1)}, bf16[64,7168]{1,0:T(8,128)(2,1)S(1)}, u32[]{:S(2)}, u32[]{:S(2)}) collective-permute-start(bf16[64,7168]{1,0:T(8,128)(2,1)S(1)} %get-tuple-element.70), channel_id=1, source_target_pairs={{0,1},{1,2},{2,3},{3,0},{4,5},{5,6},{6,7},{7,4},{8,9},{9,10},{10,1... | collective-permute-start | bytes 2752520 | tf_op jit(solution)/shard_map/ppermute | solution.py:43
  147.6 16.0 %collective-permute-start.29 = (bf16[64,7168]{1,0:T(8,128)(2,1)S(1)}, bf16[64,7168]{1,0:T(8,128)(2,1)S(1)}, u32[]{:S(2)}, u32[]{:S(2)}) collective-permute-start(bf16[64,7168]{1,0:T(8,128)(2,1)S(1)} %get-tuple-element.69), channel_id=1, source_target_pairs={{0,16},{1,17},{2,18},{3,19},{4,20},{5,21},{6,22},{7,23},{8,24},{9,... | collective-permute-start | bytes 2752520 | tf_op jit(solution)/shard_map/ppermute | solution.py:43
  161.7 32.4 %collective-permute-start.38 = (bf16[80,7168]{1,0:T(8,128)(2,1)}, bf16[80,7168]{1,0:T(8,128)(2,1)}, u32[]{:S(2)}, u32[]{:S(2)}) collective-permute-start(bf16[80,7168]{1,0:T(8,128)(2,1)} %get-tuple-element.74.refs_4_), channel_id=1, source_target_pairs={{0,4},{1,5},{2,6},{3,7},{4,8},{5,9},{6,10},{7,11},{8,12},{9,13},{1... | collective-permute-start | bytes 3440648 | tf_op jit(solution)/shard_map/ppermute | solution.py:43
  163.6 30.5 %collective-permute-start.39 = (bf16[80,7168]{1,0:T(8,128)(2,1)}, bf16[80,7168]{1,0:T(8,128)(2,1)}, u32[]{:S(2)}, u32[]{:S(2)}) collective-permute-start(bf16[80,7168]{1,0:T(8,128)(2,1)} %get-tuple-element.78), channel_id=1, source_target_pairs={{0,12},{1,13},{2,14},{3,15},{4,0},{5,1},{6,2},{7,3},{8,4},{9,5},{1... | collective-permute-start | bytes 3440648 | tf_op jit(solution)/shard_map/ppermute | solution.py:43
  165.1 24.9 %collective-permute-start.33 = (bf16[64,7168]{1,0:T(8,128)(2,1)}, bf16[64,7168]{1,0:T(8,128)(2,1)}, u32[]{:S(2)}, u32[]{:S(2)}) collective-permute-start(bf16[64,7168]{1,0:T(8,128)(2,1)} %shard_map.110.mine_ref), channel_id=1, source_target_pairs={{0,64},{1,65},{2,66},{3,67},{4,68},{5,69},{6,70},{7,71},{8,72},{9,... | collective-permute-start | bytes 2752520 | tf_op jit(solution)/shard_map/ppermute | solution.py:43
  173.8 15.6 %collective-permute-start.37 = (f32[1,7168]{1,0:T(1,128)S(1)}, f32[1,7168]{1,0:T(1,128)S(1)}, u32[]{:S(2)}, u32[]{:S(2)}) collective-permute-start(f32[1,7168]{1,0:T(1,128)S(1)} %add.324), channel_id=1, source_target_pairs={{0,64},{1,65},{2,66},{3,67},{4,68},{5,69},{6,70},{7,71},{8,72},{9,... | collective-permute-start | bytes 86024 | tf_op jit(solution)/shard_map/ppermute | solution.py:43
  (50 other events, 420.0 us)

commit v3 on v2

--- a/solution.py
+++ b/solution.py
@@ -392,37 +392,41 @@
     )
     head_far = along_z(head_far, 1)
 
-    sum_after, flip_own, gain_sum = by_strips(
+    sum_after, flip_own, head_before, gain_sum = by_strips(
         lambda after, f_after, far, own, before: (wide(after) + wide(f_after) + wide(far), wide(own) + wide(before)),
         all_rows(sum_after, flip_after, sum_far, flip_own, flip_before),
         [(part, half), (part, half)],
         after=[sum_before],
-        passed=[gain_sum],
+        passed=[head_before, gain_sum],
     )
     sum_after = along_y(sum_after, 1)
     flip_own = flip_x(flip_own)
+    head_before = along_z(head_before, -1)
     gain_other = move(gain_sum, lambda x, core, z, y: (x ^ 1, core, z, y))
 
-    head_after, gain_sum, head_before = by_strips(
-        lambda mine, theirs, far, g_sum, g_other: (mine + wide(theirs) + wide(far), g_sum + g_other),
-        [(near_head, held, held), (other_head, held, held)] + all_rows(head_far, gain_sum, gain_other),
-        [(held, half), (1, jnp.float32)],
-        after=[sum_after],
-        passed=[head_before],
+    (gain_sum,) = by_strips(
+        lambda mine, theirs: (mine + theirs,), all_rows(gain_sum, gain_other), [(1, jnp.float32)]
     )
 
     (summed,) = by_strips(
         lambda a, b, c, d: (wide(a) + wide(b) + (wide(c) + wide(d)),),
         all_rows(sum_own, flip_own, sum_after, sum_before),
         [(part, half)],
-        after=[head_after],
-    )
-    head_after, head_before = along_z(head_after, 1), along_z(head_before, -1)
+        after=[gain_sum],
+    )
+    gain_other = move(gain_sum, lambda x, core, z, y: (x, core, z, y ^ 1))
+    (head_after,) = by_strips(
+        lambda mine, theirs, far: (mine + wide(theirs) + wide(far),),
+        [(near_head, held, held), (other_head, held, held), (head_far, 0, held)],
+        [(held, half)],
+        after=[summed, gain_other],
+    )
+    head_after = along_z(head_after, 1)
     grad_hidden, placed = hidden_grads(summed, along_x(summed, 2), hidden, gain, core, [])
     other_half = along_core(grad_hidden)
     grad_hidden = lax.dynamic_update_slice(placed, other_half, ((1 - core) * part, 0))
 
-    gain_sum = gain_sum + move(gain_sum, lambda x, core, z, y: (x, core, z, y ^ 1))
+    gain_sum = gain_sum + gain_other
     gain_sum = gain_sum + move(gain_sum, lambda x, core, z, y: (x, core, z, y + 2))
     grad_gain = gain_sum + along_x(gain_sum, 2)
     grad_gain = grad_gain.reshape(width) / gain

time: 202 us -> 201 us (level)
    unnamed x68 -> x66, local copies, waits for them, and re-layouts: 15 us -> 16.5 us
    pallas_call x5 -> x6, Pallas kernels: 6.3 us -> 4.88 us  [by_strips(): pl.pallas_call(kernel, grid=(width // block,), in_specs=[strip(rows, star...]
  transfers between devices with their start and end apart: 40 -> 40, of which waited for: 22 -> 22; matrix products, arithmetic and copies ran while one was open for 4% -> 4% of each run, Pallas kernels for 14% -> 13%
where the time goes in v3:
time: 201 us; the launch traced here: 200 us
  waiting for transfers between devices  72.2 us (36%)
  starting transfers between devices  56.6 us (28%)
  Pallas kernels  44.4 us (22%)
  local copies, waits for them, and re-layouts  16.9 us (8%)
  other arithmetic  8.74 us (4%)
    ppermute x40, waiting for transfers between devices, move(): return lax.ppermute(array, AXES, pairs)  72.2 us
    ppermute x40, starting transfers between devices, move(): return lax.ppermute(array, AXES, pairs)  56.6 us
    unnamed x66, local copies, waits for them, and re-layouts  16.5 us
    pallas_call x2, Pallas kernels, all_logits(): pl.pallas_call(lambda *refs: logits_kernel(len(head), len(tokens), *refs)...  14.3 us
    pallas_call x1, Pallas kernels, token_grads(): pl.pallas_call(lambda *refs: token_grad_kernel(len(head), part, *refs), g...  11.5 us
    pallas_call x1, Pallas kernels, head_grads(): pl.pallas_call(lambda *refs: head_grad_kernel(len(head), len(tokens), *re...  10 us
    convert_element_type x1, other arithmetic, adam_step(): (wfloat - 0.001 * update).astype(jnp.bfloat16)  5.79 us
    pallas_call x6, Pallas kernels, by_strips(): pl.pallas_call(kernel, grid=(width // block,), in_specs=[strip(rows, star...  4.88 us
  transfers between devices with their start and end apart: 40, of which 22 were waited for; matrix products, arithmetic and copies ran while one was open for 4% of the time, Pallas kernels for 13%

profile of v3, /device:TPU:1, one launch (start us, length us, event | category | flops | bytes accessed | tf_op | source)
XLA Modules:
  0.0 200.0 jit_solution(7075869245366844042)
XLA Ops:
  0.6 2.5 %collective-permute-start = (bf16[80,7168]{1,0:T(8,128)(2,1)}, bf16[80,7168]{1,0:T(8,128)(2,1)S(1)}, u32[]{:S(2)}, u32[]{:S(2)}) collective-permute-start(bf16[80,7168]{1,0:T(8,128)(2,1)} %refs_1_.1), channel_id=1, source_target_pairs={{0,12},{1,13},{2,14},{3,15},{4,0},{5,1},{6,2},{7,3},{8,4},{9,5},{1... | collective-permute-start | bytes 3440648 | tf_op jit(solution)/shard_map/ppermute | solution.py:43
  14.4 4.9 %collective-permute-done.refs_1_.refs_5_.refs_2_ = bf16[80,7168]{1,0:T(8,128)(2,1)S(1)} collective-permute-done((bf16[80,7168]{1,0:T(8,128)(2,1)}, bf16[80,7168]{1,0:T(8,128)(2,1)S(1)}, u32[]{:S(2)}, u32[]{:S(2)}) %collective-permute-start) | collective-permute-done | bytes 1146912 | tf_op jit(solution)/shard_map/ppermute | solution.py:43
  20.8 3.6 %collective-permute-done.7.refs_9_.refs_15_.refs_10_ = bf16[64,7296]{1,0:T(8,128)(2,1)S(1)} collective-permute-done((bf16[64,7296]{1,0:T(8,128)(2,1)S(1)}, bf16[64,7296]{1,0:T(8,128)(2,1)S(1)}, u32[]{:S(2)}, u32[]{:S(2)}) %collective-permute-start.7) | collective-permute-done | bytes 933920 | tf_op jit(solution)/shard_map/ppermute | solution.py:43
  24.4 4.3 %collective-permute-done.8.refs_11_.refs_17_.refs_12_ = bf16[64,7296]{1,0:T(8,128)(2,1)S(1)} collective-permute-done((bf16[64,7296]{1,0:T(8,128)(2,1)S(1)}, bf16[64,7296]{1,0:T(8,128)(2,1)S(1)}, u32[]{:S(2)}, u32[]{:S(2)}) %collective-permute-start.8) | collective-permute-done | bytes 933920 | tf_op jit(solution)/shard_map/ppermute | solution.py:43
  30.9 4.3 %collective-permute-start.3 = (bf16[80,7168]{1,0:T(8,128)(2,1)S(1)}, bf16[80,7168]{1,0:T(8,128)(2,1)S(1)}, u32[]{:S(2)}, u32[]{:S(2)}) collective-permute-start(bf16[80,7168]{1,0:T(8,128)(2,1)S(1)} %copy-done.2), channel_id=1, source_target_pairs={{0,32},{1,33},{2,34},{3,35},{4,36},{5,37},{6,38},{7,39},{8,40},{9,... | collective-permute-start | bytes 3440648 | tf_op jit(solution)/shard_map/ppermute | solution.py:43
  38.7 4.9 %collective-permute-done.10.refs_10_.refs_16_.refs_11_ = bf16[64,7296]{1,0:T(8,128)(2,1)} collective-permute-done((bf16[64,7296]{1,0:T(8,128)(2,1)S(1)}, bf16[64,7296]{1,0:T(8,128)(2,1)}, u32[]{:S(2)}, u32[]{:S(2)}) %collective-permute-start.10) | collective-permute-done | bytes 933920 | tf_op jit(solution)/shard_map/ppermute | solution.py:43
  43.6 2.8 %collective-permute-start.6 = (bf16[80,7168]{1,0:T(8,128)(2,1)}, bf16[80,7168]{1,0:T(8,128)(2,1)}, u32[]{:S(2)}, u32[]{:S(2)}) collective-permute-start(bf16[80,7168]{1,0:T(8,128)(2,1)} %collective-permute-done.2.refs_3_.refs_7_.refs_4_), channel_id=1, source_target_pairs={{0,32},{1,33},{2,34},{3,35},{4,36},{5,37},{6,38},{7,39},{8,40},{9,... | collective-permute-start | bytes 3440648 | tf_op jit(solution)/shard_map/ppermute | solution.py:43
  59.2 8.5 %shard_map.102 = (f32[640,384]{1,0:T(8,128)S(1)}, f32[3,384]{1,0:T(4,128)S(1)}) custom-call(bf16[80,7168]{1,0:T(8,128)(2,1)S(1)} %copy-done.2, bf16[80,7168]{1,0:T(8,128)(2,1)S(1)} %collective-permute-done.refs_1_.refs_5_.refs_2_, bf16[80,7168]{1,0:T(8,128)(2,1)} %collective-permute-done.1.refs_2_.refs_6_.refs_3_, ...), custom_call_target="tpu_custom_call" | custom-call | flops 3523215360 | bytes 14680064 | tf_op jit(solution)/shard_map/pallas_call | solution.py:202
  68.6 5.8 %shard_map.103 = (f32[640,128]{1,0:T(8,128)S(1)}, f32[3,128]{1,0:T(4,128)S(1)}) custom-call(bf16[80,7168]{1,0:T(8,128)(2,1)S(1)} %copy-done.2, bf16[80,7168]{1,0:T(8,128)(2,1)S(1)} %collective-permute-done.refs_1_.refs_5_.refs_2_, bf16[80,7168]{1,0:T(8,128)(2,1)} %collective-permute-done.1.refs_2_.refs_6_.refs_3_, ...), custom_call_target="tpu_custom_call" | custom-call | flops 1174405120 | bytes 11010048 | tf_op jit(solution)/shard_map/pallas_call | solution.py:202
  82.2 2.7 %collective-permute-start.19 = (f32[2,2,4,64]{3,2,1,0:T(4,128)S(1)}, f32[2,2,4,64]{3,2,1,0:T(4,128)S(1)}, u32[]{:S(2)}, u32[]{:S(2)}) collective-permute-start(f32[2,2,4,64]{3,2,1,0:T(4,128)S(1)} %get-tuple-element.79), channel_id=1, source_target_pairs={{0,80},{1,81},{2,82},{3,83},{4,84},{5,85},{6,86},{7,87},{8,88},{9,... | collective-permute-start | bytes 12296 | tf_op jit(solution)/shard_map/ppermute | solution.py:43
  85.6 3.2 %collective-permute-done.18 = f32[2,2,4,64]{3,2,1,0:T(4,128)S(1)} collective-permute-done((f32[2,2,4,64]{3,2,1,0:T(4,128)S(1)}, f32[2,2,4,64]{3,2,1,0:T(4,128)S(1)}, u32[]{:S(2)}, u32[]{:S(2)}) %collective-permute-start.18) | collective-permute-done | bytes 4128 | tf_op jit(solution)/shard_map/ppermute | solution.py:43
  89.7 11.5 %shard_map.104 = (bf16[640,512]{1,0:T(8,128)(2,1)}, bf16[64,7168]{1,0:T(8,128)(2,1)}, bf16[64,7168]{1,0:T(8,128)(2,1)}, bf16[64,7168]{1,0:T(8,128)(2,1)}, bf16[6...) custom-call(f32[640,384]{1,0:T(8,128)} %copy-done.27, ...), custom_call_target="tpu_custom_call" | custom-call | flops 4697620480 | bytes 16515072 | tf_op jit(solution)/shard_map/pallas_call | solution.py:241
  102.5 10.0 %shard_map.105 = (f32[320,7168]{1,0:T(8,128)}, bf16[320,7168]{1,0:T(8,128)(2,1)S(1)}, f32[1,7168]{1,0:T(1,128)S(1)}) custom-call(bf16[640,512]{1,0:T(8,128)(2,1)S(1)} %copy-done.29, bf16[80,7168]{1,0:T(8,128)(2,1)S(1)} %copy-done.3, bf16[80,7168]{1,0:T(8,128)(2,1)S(1)} %copy-done.7, bf16[80,7168]{1,0:T(8,128)(2,1)} %collective-permute-done.1.refs_2_.refs_6_.refs_3_, ...), custom_call_target="tpu_custom_call" | custom-call | flops 4697620480 | bytes 16515072 | tf_op jit(solution)/shard_map/pallas_call | solution.py:266
  115.7 3.4 %collective-permute-start.25 = (bf16[320,7168]{1,0:T(8,128)(2,1)S(1)}, bf16[320,7168]{1,0:T(8,128)(2,1)S(1)}, u32[]{:S(2)}, u32[]{:S(2)}) collective-permute-start(bf16[320,7168]{1,0:T(8,128)(2,1)S(1)} %get-tuple-element.64), channel_id=1, source_target_pairs={{0,32},{1,33},{2,34},{3,35},{4,36},{5,37},{6,38},{7,39},{8,40},{9,... | collective-permute-start | bytes 13762568 | tf_op jit(solution)/shard_map/ppermute | solution.py:43
  120.9 3.2 %collective-permute-start.23 = (bf16[64,7168]{1,0:T(8,128)(2,1)S(1)}, bf16[64,7168]{1,0:T(8,128)(2,1)S(1)}, u32[]{:S(2)}, u32[]{:S(2)}) collective-permute-start(bf16[64,7168]{1,0:T(8,128)(2,1)S(1)} %get-tuple-element.60), channel_id=1, source_target_pairs={{0,1},{1,2},{2,3},{3,0},{4,5},{5,6},{6,7},{7,4},{8,9},{9,10},{10,1... | collective-permute-start | bytes 2752520 | tf_op jit(solution)/shard_map/ppermute | solution.py:43
  127.1 2.9 %collective-permute-start.27 = (f32[1,7168]{1,0:T(1,128)S(1)}, f32[1,7168]{1,0:T(1,128)S(1)}, u32[]{:S(2)}, u32[]{:S(2)}) collective-permute-start(f32[1,7168]{1,0:T(1,128)S(1)} %add.320), channel_id=1, source_target_pairs={{0,8},{1,9},{2,10},{3,11},{4,12},{5,13},{6,14},{7,15},{8,0},{9,1},... | collective-permute-start | bytes 86024 | tf_op jit(solution)/shard_map/ppermute | solution.py:43
  137.1 5.9 %collective-permute-done.23.refs_2_ = bf16[64,7168]{1,0:T(8,128)(2,1)S(1)} collective-permute-done((bf16[64,7168]{1,0:T(8,128)(2,1)S(1)}, bf16[64,7168]{1,0:T(8,128)(2,1)S(1)}, u32[]{:S(2)}, u32[]{:S(2)}) %collective-permute-start.23) | collective-permute-done | bytes 917536 | tf_op jit(solution)/shard_map/ppermute | solution.py:43
  144.5 2.8 %collective-permute-start.29 = (bf16[64,7168]{1,0:T(8,128)(2,1)S(1)}, bf16[64,7168]{1,0:T(8,128)(2,1)S(1)}, u32[]{:S(2)}, u32[]{:S(2)}) collective-permute-start(bf16[64,7168]{1,0:T(8,128)(2,1)S(1)} %get-tuple-element.68), channel_id=1, source_target_pairs={{0,16},{1,17},{2,18},{3,19},{4,20},{5,21},{6,22},{7,23},{8,24},{9,... | collective-permute-start | bytes 2752520 | tf_op jit(solution)/shard_map/ppermute | solution.py:43
  149.0 8.7 %collective-permute-done.31.refs_1_ = f32[1,7168]{1,0:T(1,128)S(1)} collective-permute-done((f32[1,7168]{1,0:T(1,128)S(1)}, f32[1,7168]{1,0:T(1,128)S(1)}, u32[]{:S(2)}, u32[]{:S(2)}) %collective-permute-start.31) | collective-permute-done | bytes 28704 | tf_op jit(solution)/shard_map/ppermute | solution.py:43
  163.3 3.0 %collective-permute-start.32 = (bf16[64,7168]{1,0:T(8,128)(2,1)S(1)}, bf16[64,7168]{1,0:T(8,128)(2,1)}, u32[]{:S(2)}, u32[]{:S(2)}) collective-permute-start(bf16[64,7168]{1,0:T(8,128)(2,1)S(1)} %shard_map.110.mine_ref.refs_3_), channel_id=1, source_target_pairs={{0,64},{1,65},{2,66},{3,67},{4,68},{5,69},{6,70},{7,71},{8,72},{9,... | collective-permute-start | bytes 2752520 | tf_op jit(solution)/shard_map/ppermute | solution.py:43
  166.5 4.7 %collective-permute-done.35 = f32[1,7168]{1,0:T(1,128)S(1)} collective-permute-done((f32[1,7168]{1,0:T(1,128)S(1)}, f32[1,7168]{1,0:T(1,128)S(1)}, u32[]{:S(2)}, u32[]{:S(2)}) %collective-permute-start.35) | collective-permute-done | bytes 28704 | tf_op jit(solution)/shard_map/ppermute | solution.py:43
  171.4 15.8 %collective-permute-done.36 = f32[1,7168]{1,0:T(1,128)S(1)} collective-permute-done((f32[1,7168]{1,0:T(1,128)S(1)}, f32[1,7168]{1,0:T(1,128)S(1)}, u32[]{:S(2)}, u32[]{:S(2)}) %collective-permute-start.36) | collective-permute-done | bytes 28704 | tf_op jit(solution)/shard_map/ppermute | solution.py:43
  189.3 3.1 %shard_map.111 = (bf16[64,7168]{1,0:T(8,128)(2,1)S(1)}, bf16[128,7168]{1,0:T(8,128)(2,1)}) custom-call(s32[1]{0:T(128)} %bitcast.core_ref, bf16[64,7168]{1,0:T(8,128)(2,1)S(1)} %shard_map.110.mine_ref.refs_3_, bf16[64,7168]{1,0:T(8,128)(2,1)} %collective-permute-done.32.their_ref, bf16[128,7168]{1,0:T(8,128)(2,1)S(1)} %copy-done.5, f32[1,7168]{1,0:T(1,128)S(1)} %bitcast.50), custom_call_target="tpu_custom_call" | custom-call | bytes 3670016 | tf_op jit(solution)/shard_map/pallas_call | solution.py:294
  192.9 5.8 %fusion.2 = (bf16[80,7168]{1,0:T(8,128)(2,1)}, f32[80,7168]{1,0:T(8,128)}, f32[80,7168]{1,0:T(8,128)}) fusion(bf16[80,7168]{1,0:T(8,128)(2,1)S(1)} %copy-done.3, bf16[80,7168]{1,0:T(8,128)(2,1)} %collective-permute-done.39, bf16[80,7168]{1,0:T(8,128)(2,1)} %collective-permute-done.38, bf16[320,7168]{1,0:T(8,128)(2,1)} %copy-done.1, ...), kind=kLoop, calls=%fused_computation.5 | loop fusion | flops 13189120 | bytes 17203200 | tf_op jit(solution)/shard_map/convert_element_type | solution.py:25
  (174 shorter events, 70.4 us)
Async XLA Ops:
  0.6 18.7 %collective-permute-start = (bf16[80,7168]{1,0:T(8,128)(2,1)}, bf16[80,7168]{1,0:T(8,128)(2,1)S(1)}, u32[]{:S(2)}, u32[]{:S(2)}) collective-permute-start(bf16[80,7168]{1,0:T(8,128)(2,1)} %refs_1_.1), channel_id=1, source_target_pairs={{0,12},{1,13},{2,14},{3,15},{4,0},{5,1},{6,2},{7,3},{8,4},{9,5},{1... | collective-permute-start | bytes 3440648 | tf_op jit(solution)/shard_map/ppermute | solution.py:43
  6.8 17.6 %collective-permute-start.7 = (bf16[64,7296]{1,0:T(8,128)(2,1)S(1)}, bf16[64,7296]{1,0:T(8,128)(2,1)S(1)}, u32[]{:S(2)}, u32[]{:S(2)}) collective-permute-start(bf16[64,7296]{1,0:T(8,128)(2,1)S(1)} %shard_map.101.refs_8_.refs_14_.refs_9_), channel_id=1, source_target_pairs={{0,3},{1,0},{2,1},{3,2},{4,7},{5,4},{6,5},{7,6},{8,11},{9,8},{10,9... | collective-permute-start | bytes 2801672 | tf_op jit(solution)/shard_map/ppermute | solution.py:43
  8.2 20.5 %collective-permute-start.8 = (bf16[64,7296]{1,0:T(8,128)(2,1)S(1)}, bf16[64,7296]{1,0:T(8,128)(2,1)S(1)}, u32[]{:S(2)}, u32[]{:S(2)}) collective-permute-start(bf16[64,7296]{1,0:T(8,128)(2,1)S(1)} %shard_map.101.refs_8_.refs_14_.refs_9_), channel_id=1, source_target_pairs={{0,1},{1,2},{2,3},{3,0},{4,5},{5,6},{6,7},{7,4},{8,9},{9,10},{10,1... | collective-permute-start | bytes 2801672 | tf_op jit(solution)/shard_map/ppermute | solution.py:43
  9.7 20.0 %collective-permute-start.9 = (bf16[64,7296]{1,0:T(8,128)(2,1)S(1)}, bf16[64,7296]{1,0:T(8,128)(2,1)}, u32[]{:S(2)}, u32[]{:S(2)}) collective-permute-start(bf16[64,7296]{1,0:T(8,128)(2,1)S(1)} %shard_map.101.refs_8_.refs_14_.refs_9_), channel_id=1, source_target_pairs={{0,16},{1,17},{2,18},{3,19},{4,20},{5,21},{6,22},{7,23},{8,24},{9,... | collective-permute-start | bytes 2801672 | tf_op jit(solution)/shard_map/ppermute | solution.py:43
  12.2 26.6 %collective-permute-start.2 = (bf16[80,7168]{1,0:T(8,128)(2,1)S(1)}, bf16[80,7168]{1,0:T(8,128)(2,1)}, u32[]{:S(2)}, u32[]{:S(2)}) collective-permute-start(bf16[80,7168]{1,0:T(8,128)(2,1)S(1)} %copy-done.2), channel_id=1, source_target_pairs={{0,4},{1,5},{2,6},{3,7},{4,8},{5,9},{6,10},{7,11},{8,12},{9,13},{1... | collective-permute-start | bytes 3440648 | tf_op jit(solution)/shard_map/ppermute | solution.py:43
  19.3 27.0 %collective-permute-start.1 = (bf16[80,7168]{1,0:T(8,128)(2,1)S(1)}, bf16[80,7168]{1,0:T(8,128)(2,1)}, u32[]{:S(2)}, u32[]{:S(2)}) collective-permute-start(bf16[80,7168]{1,0:T(8,128)(2,1)S(1)} %collective-permute-done.refs_1_.refs_5_.refs_2_), channel_id=1, source_target_pairs={{0,12},{1,13},{2,14},{3,15},{4,0},{5,1},{6,2},{7,3},{8,4},{9,5},{1... | collective-permute-start | bytes 3440648 | tf_op jit(solution)/shard_map/ppermute | solution.py:43
  29.6 13.9 %collective-permute-start.10 = (bf16[64,7296]{1,0:T(8,128)(2,1)S(1)}, bf16[64,7296]{1,0:T(8,128)(2,1)}, u32[]{:S(2)}, u32[]{:S(2)}) collective-permute-start(bf16[64,7296]{1,0:T(8,128)(2,1)S(1)} %collective-permute-done.7.refs_9_.refs_15_.refs_10_), channel_id=1, source_target_pairs={{0,3},{1,0},{2,1},{3,2},{4,7},{5,4},{6,5},{7,6},{8,11},{9,8},{10,9... | collective-permute-start | bytes 2801672 | tf_op jit(solution)/shard_map/ppermute | solution.py:43
  30.9 19.9 %collective-permute-start.3 = (bf16[80,7168]{1,0:T(8,128)(2,1)S(1)}, bf16[80,7168]{1,0:T(8,128)(2,1)S(1)}, u32[]{:S(2)}, u32[]{:S(2)}) collective-permute-start(bf16[80,7168]{1,0:T(8,128)(2,1)S(1)} %copy-done.2), channel_id=1, source_target_pairs={{0,32},{1,33},{2,34},{3,35},{4,36},{5,37},{6,38},{7,39},{8,40},{9,... | collective-permute-start | bytes 3440648 | tf_op jit(solution)/shard_map/ppermute | solution.py:43
  35.3 13.0 %collective-permute-start.11 = (bf16[64,7296]{1,0:T(8,128)(2,1)S(1)}, bf16[64,7296]{1,0:T(8,128)(2,1)S(1)}, u32[]{:S(2)}, u32[]{:S(2)}) collective-permute-start(bf16[64,7296]{1,0:T(8,128)(2,1)S(1)} %collective-permute-done.7.refs_9_.refs_15_.refs_10_), channel_id=1, source_target_pairs={{0,16},{1,17},{2,18},{3,19},{4,20},{5,21},{6,22},{7,23},{8,24},{9,... | collective-permute-start | bytes 2801672 | tf_op jit(solution)/shard_map/ppermute | solution.py:43
  38.7 15.6 %collective-permute-start.4 = (bf16[80,7168]{1,0:T(8,128)(2,1)S(1)}, bf16[80,7168]{1,0:T(8,128)(2,1)}, u32[]{:S(2)}, u32[]{:S(2)}) collective-permute-start(bf16[80,7168]{1,0:T(8,128)(2,1)S(1)} %collective-permute-done.refs_1_.refs_5_.refs_2_), channel_id=1, source_target_pairs={{0,32},{1,33},{2,34},{3,35},{4,36},{5,37},{6,38},{7,39},{8,40},{9,... | collective-permute-start | bytes 3440648 | tf_op jit(solution)/shard_map/ppermute | solution.py:43
  49.2 19.4 %collective-permute-start.13 = (bf16[64,7296]{1,0:T(8,128)(2,1)}, bf16[64,7296]{1,0:T(8,128)(2,1)}, u32[]{:S(2)}, u32[]{:S(2)}) collective-permute-start(bf16[64,7296]{1,0:T(8,128)(2,1)} %collective-permute-done.9.refs_12_.refs_18_.refs_13_), channel_id=1, source_target_pairs={{0,1},{1,2},{2,3},{3,0},{4,5},{5,6},{6,7},{7,4},{8,9},{9,10},{10,1... | collective-permute-start | bytes 2801672 | tf_op jit(solution)/shard_map/ppermute | solution.py:43
  51.8 16.8 %collective-permute-start.12 = (bf16[64,7296]{1,0:T(8,128)(2,1)}, bf16[64,7296]{1,0:T(8,128)(2,1)}, u32[]{:S(2)}, u32[]{:S(2)}) collective-permute-start(bf16[64,7296]{1,0:T(8,128)(2,1)} %collective-permute-done.10.refs_10_.refs_16_.refs_11_), channel_id=1, source_target_pairs={{0,16},{1,17},{2,18},{3,19},{4,20},{5,21},{6,22},{7,23},{8,24},{9,... | collective-permute-start | bytes 2801672 | tf_op jit(solution)/shard_map/ppermute | solution.py:43
  101.2 14.0 %collective-permute-start.21 = (bf16[64,7168]{1,0:T(8,128)(2,1)}, bf16[64,7168]{1,0:T(8,128)(2,1)S(1)}, u32[]{:S(2)}, u32[]{:S(2)}) collective-permute-start(bf16[64,7168]{1,0:T(8,128)(2,1)} %get-tuple-element.55), channel_id=1, source_target_pairs={{0,3},{1,0},{2,1},{3,2},{4,7},{5,4},{6,5},{7,6},{8,11},{9,8},{10,9... | collective-permute-start | bytes 2752520 | tf_op jit(solution)/shard_map/ppermute | solution.py:43
  115.7 17.4 %collective-permute-start.25 = (bf16[320,7168]{1,0:T(8,128)(2,1)S(1)}, bf16[320,7168]{1,0:T(8,128)(2,1)S(1)}, u32[]{:S(2)}, u32[]{:S(2)}) collective-permute-start(bf16[320,7168]{1,0:T(8,128)(2,1)S(1)} %get-tuple-element.64), channel_id=1, source_target_pairs={{0,32},{1,33},{2,34},{3,35},{4,36},{5,37},{6,38},{7,39},{8,40},{9,... | collective-permute-start | bytes 13762568 | tf_op jit(solution)/shard_map/ppermute | solution.py:43
  119.1 17.9 %collective-permute-start.22 = (bf16[64,7168]{1,0:T(8,128)(2,1)}, bf16[64,7168]{1,0:T(8,128)(2,1)S(1)}, u32[]{:S(2)}, u32[]{:S(2)}) collective-permute-start(bf16[64,7168]{1,0:T(8,128)(2,1)} %get-tuple-element.59), channel_id=1, source_target_pairs={{0,16},{1,17},{2,18},{3,19},{4,20},{5,21},{6,22},{7,23},{8,24},{9,... | collective-permute-start | bytes 2752520 | tf_op jit(solution)/shard_map/ppermute | solution.py:43
  120.9 22.1 %collective-permute-start.23 = (bf16[64,7168]{1,0:T(8,128)(2,1)S(1)}, bf16[64,7168]{1,0:T(8,128)(2,1)S(1)}, u32[]{:S(2)}, u32[]{:S(2)}) collective-permute-start(bf16[64,7168]{1,0:T(8,128)(2,1)S(1)} %get-tuple-element.60), channel_id=1, source_target_pairs={{0,1},{1,2},{2,3},{3,0},{4,5},{5,6},{6,7},{7,4},{8,9},{9,10},{10,1... | collective-permute-start | bytes 2752520 | tf_op jit(solution)/shard_map/ppermute | solution.py:43
  124.1 19.4 %collective-permute-start.24 = (bf16[64,7168]{1,0:T(8,128)(2,1)S(1)}, bf16[64,7168]{1,0:T(8,128)(2,1)S(1)}, u32[]{:S(2)}, u32[]{:S(2)}) collective-permute-start(bf16[64,7168]{1,0:T(8,128)(2,1)S(1)} %get-tuple-element.62), channel_id=1, source_target_pairs={{0,3},{1,0},{2,1},{3,2},{4,7},{5,4},{6,5},{7,6},{8,11},{9,8},{10,9... | collective-permute-start | bytes 2752520 | tf_op jit(solution)/shard_map/ppermute | solution.py:43
  135.0 26.1 %collective-permute-start.37 = (bf16[80,7168]{1,0:T(8,128)(2,1)S(1)}, bf16[80,7168]{1,0:T(8,128)(2,1)S(1)}, u32[]{:S(2)}, u32[]{:S(2)}) collective-permute-start(bf16[80,7168]{1,0:T(8,128)(2,1)S(1)} %get-tuple-element.73), channel_id=1, source_target_pairs={{0,4},{1,5},{2,6},{3,7},{4,8},{5,9},{6,10},{7,11},{8,12},{9,13},{1... | collective-permute-start | bytes 3440648 | tf_op jit(solution)/shard_map/ppermute | solution.py:43
  144.5 14.1 %collective-permute-start.29 = (bf16[64,7168]{1,0:T(8,128)(2,1)S(1)}, bf16[64,7168]{1,0:T(8,128)(2,1)S(1)}, u32[]{:S(2)}, u32[]{:S(2)}) collective-permute-start(bf16[64,7168]{1,0:T(8,128)(2,1)S(1)} %get-tuple-element.68), channel_id=1, source_target_pairs={{0,16},{1,17},{2,18},{3,19},{4,20},{5,21},{6,22},{7,23},{8,24},{9,... | collective-permute-start | bytes 2752520 | tf_op jit(solution)/shard_map/ppermute | solution.py:43
  147.3 12.9 %collective-permute-start.30 = (bf16[64,7168]{1,0:T(8,128)(2,1)S(1)}, bf16[64,7168]{1,0:T(8,128)(2,1)S(1)}, u32[]{:S(2)}, u32[]{:S(2)}) collective-permute-start(bf16[64,7168]{1,0:T(8,128)(2,1)S(1)} %get-tuple-element.69), channel_id=1, source_target_pairs={{0,1},{1,2},{2,3},{3,0},{4,5},{5,6},{6,7},{7,4},{8,9},{9,10},{10,1... | collective-permute-start | bytes 2752520 | tf_op jit(solution)/shard_map/ppermute | solution.py:43
  157.9 35.0 %collective-permute-start.39 = (bf16[80,7168]{1,0:T(8,128)(2,1)}, bf16[80,7168]{1,0:T(8,128)(2,1)}, u32[]{:S(2)}, u32[]{:S(2)}) collective-permute-start(bf16[80,7168]{1,0:T(8,128)(2,1)} %get-tuple-element.74), channel_id=1, source_target_pairs={{0,12},{1,13},{2,14},{3,15},{4,0},{5,1},{6,2},{7,3},{8,4},{9,5},{1... | collective-permute-start | bytes 3440648 | tf_op jit(solution)/shard_map/ppermute | solution.py:43
  161.9 31.0 %collective-permute-start.38 = (bf16[80,7168]{1,0:T(8,128)(2,1)S(1)}, bf16[80,7168]{1,0:T(8,128)(2,1)}, u32[]{:S(2)}, u32[]{:S(2)}) collective-permute-start(bf16[80,7168]{1,0:T(8,128)(2,1)S(1)} %shard_map.112), channel_id=1, source_target_pairs={{0,4},{1,5},{2,6},{3,7},{4,8},{5,9},{6,10},{7,11},{8,12},{9,13},{1... | collective-permute-start | bytes 3440648 | tf_op jit(solution)/shard_map/ppermute | solution.py:43
  163.3 24.5 %collective-permute-start.32 = (bf16[64,7168]{1,0:T(8,128)(2,1)S(1)}, bf16[64,7168]{1,0:T(8,128)(2,1)}, u32[]{:S(2)}, u32[]{:S(2)}) collective-permute-start(bf16[64,7168]{1,0:T(8,128)(2,1)S(1)} %shard_map.110.mine_ref.refs_3_), channel_id=1, source_target_pairs={{0,64},{1,65},{2,66},{3,67},{4,68},{5,69},{6,70},{7,71},{8,72},{9,... | collective-permute-start | bytes 2752520 | tf_op jit(solution)/shard_map/ppermute | solution.py:43
  171.3 15.9 %collective-permute-start.36 = (f32[1,7168]{1,0:T(1,128)S(1)}, f32[1,7168]{1,0:T(1,128)S(1)}, u32[]{:S(2)}, u32[]{:S(2)}) collective-permute-start(f32[1,7168]{1,0:T(1,128)S(1)} %add.324), channel_id=1, source_target_pairs={{0,64},{1,65},{2,66},{3,67},{4,68},{5,69},{6,70},{7,71},{8,72},{9,... | collective-permute-start | bytes 86024 | tf_op jit(solution)/shard_map/ppermute | solution.py:43
  (49 other events, 379.0 us)

commit v4 on v3

--- a/solution.py
+++ b/solution.py
@@ -81,8 +81,8 @@
     return jnp.stack([top, total])
 
 
-def strips(pieces):
-    return [pl.BlockSpec((piece.shape[0], BLOCK), lambda i: (0, i)) for piece in pieces]
+def strips(pieces, block=BLOCK):
+    return [pl.BlockSpec((piece.shape[0], block), lambda i: (0, i)) for piece in pieces]
 
 
 def whole(shape):
@@ -201,8 +201,8 @@
     digits = [pl.BlockSpec((piece.shape[0], LANES), lambda i: (0, width // LANES)) for piece in tokens]
     return pl.pallas_call(
         lambda *refs: logits_kernel(len(head), len(tokens), *refs),
-        grid=(width // BLOCK,),
-        in_specs=strips(head) + strips(tokens) + digits + anywhere(after),
+        grid=(width // (2 * BLOCK),),
+        in_specs=strips(head, 2 * BLOCK) + strips(tokens, 2 * BLOCK) + digits + anywhere(after),
         out_specs=[whole((rows, columns)), whole((3, columns))],
         out_shape=[
             jax.ShapeDtypeStruct((rows, columns), jnp.float32),
@@ -240,9 +240,9 @@
     width, part = head[0].shape[1], columns // 8
     return pl.pallas_call(
         lambda *refs: token_grad_kernel(len(head), part, *refs),
-        grid=(width // BLOCK,),
-        in_specs=[whole(near.shape), whole(flip.shape), whole((2, columns)), whole((1, columns))] + strips(head),
-        out_specs=[whole((rows, columns))] + [pl.BlockSpec((part, BLOCK), lambda i: (0, i))] * 8,
+        grid=(width // (2 * BLOCK),),
+        in_specs=[whole(near.shape), whole(flip.shape), whole((2, columns)), whole((1, columns))] + strips(head, 2 * BLOCK),
+        out_specs=[whole((rows, columns))] + [pl.BlockSpec((part, 2 * BLOCK), lambda i: (0, i))] * 8,
         out_shape=[jax.ShapeDtypeStruct((rows, columns), half)] + [jax.ShapeDtypeStruct((part, width), half)] * 8,
         scratch_shapes=[pltpu.VMEM((columns, rows), half)],
         compiler_params=params(56),

time: 201 us -> 201 us (level)
  starting transfers between devices: 56.6 us -> 58.7 us
    ppermute x40, starting transfers between devices: 56.6 us -> 58.7 us  [move(): return lax.ppermute(array, AXES, pairs)]
where the time goes in v4:
time: 201 us; the launch traced here: 200 us
  waiting for transfers between devices  71.6 us (36%)
  starting transfers between devices  58.7 us (29%)
  Pallas kernels  43.4 us (22%)
  local copies, waits for them, and re-layouts  16.9 us (8%)
  other arithmetic  8.71 us (4%)
    ppermute x40, waiting for transfers between devices, move(): return lax.ppermute(array, AXES, pairs)  71.6 us
    ppermute x40, starting transfers between devices, move(): return lax.ppermute(array, AXES, pairs)  58.7 us
    unnamed x66, local copies, waits for them, and re-layouts  16.5 us
    pallas_call x2, Pallas kernels, all_logits(): pl.pallas_call(lambda *refs: logits_kernel(len(head), len(tokens), *refs)...  12.8 us
    pallas_call x1, Pallas kernels, token_grads(): pl.pallas_call(lambda *refs: token_grad_kernel(len(head), part, *refs), g...  11.9 us
    pallas_call x1, Pallas kernels, head_grads(): pl.pallas_call(lambda *refs: head_grad_kernel(len(head), len(tokens), *re...  10 us
    convert_element_type x1, other arithmetic, adam_step(): (wfloat - 0.001 * update).astype(jnp.bfloat16)  5.76 us
    pallas_call x6, Pallas kernels, by_strips(): pl.pallas_call(kernel, grid=(width // block,), in_specs=[strip(rows, star...  4.88 us
  transfers between devices with their start and end apart: 40, of which 22 were waited for; matrix products, arithmetic and copies ran while one was open for 4% of the time, Pallas kernels for 13%

profile of v4, /device:TPU:1, one launch (start us, length us, event | category | flops | bytes accessed | tf_op | source)
XLA Modules:
  0.0 200.5 jit_solution(13564601219216342251)
XLA Ops:
  0.6 2.5 %collective-permute-start = (bf16[80,7168]{1,0:T(8,128)(2,1)}, bf16[80,7168]{1,0:T(8,128)(2,1)S(1)}, u32[]{:S(2)}, u32[]{:S(2)}) collective-permute-start(bf16[80,7168]{1,0:T(8,128)(2,1)} %refs_1_.1), channel_id=1, source_target_pairs={{0,12},{1,13},{2,14},{3,15},{4,0},{5,1},{6,2},{7,3},{8,4},{9,5},{1... | collective-permute-start | bytes 3440648 | tf_op jit(solution)/shard_map/ppermute | solution.py:43
  14.4 4.9 %collective-permute-done.refs_1_.refs_5_.refs_2_ = bf16[80,7168]{1,0:T(8,128)(2,1)S(1)} collective-permute-done((bf16[80,7168]{1,0:T(8,128)(2,1)}, bf16[80,7168]{1,0:T(8,128)(2,1)S(1)}, u32[]{:S(2)}, u32[]{:S(2)}) %collective-permute-start) | collective-permute-done | bytes 1146912 | tf_op jit(solution)/shard_map/ppermute | solution.py:43
  20.8 3.6 %collective-permute-done.7.refs_9_.refs_15_.refs_10_ = bf16[64,7296]{1,0:T(8,128)(2,1)S(1)} collective-permute-done((bf16[64,7296]{1,0:T(8,128)(2,1)S(1)}, bf16[64,7296]{1,0:T(8,128)(2,1)S(1)}, u32[]{:S(2)}, u32[]{:S(2)}) %collective-permute-start.7) | collective-permute-done | bytes 933920 | tf_op jit(solution)/shard_map/ppermute | solution.py:43
  24.4 4.3 %collective-permute-done.8.refs_11_.refs_17_.refs_12_ = bf16[64,7296]{1,0:T(8,128)(2,1)S(1)} collective-permute-done((bf16[64,7296]{1,0:T(8,128)(2,1)S(1)}, bf16[64,7296]{1,0:T(8,128)(2,1)S(1)}, u32[]{:S(2)}, u32[]{:S(2)}) %collective-permute-start.8) | collective-permute-done | bytes 933920 | tf_op jit(solution)/shard_map/ppermute | solution.py:43
  30.9 4.3 %collective-permute-start.3 = (bf16[80,7168]{1,0:T(8,128)(2,1)S(1)}, bf16[80,7168]{1,0:T(8,128)(2,1)S(1)}, u32[]{:S(2)}, u32[]{:S(2)}) collective-permute-start(bf16[80,7168]{1,0:T(8,128)(2,1)S(1)} %copy-done.2), channel_id=1, source_target_pairs={{0,32},{1,33},{2,34},{3,35},{4,36},{5,37},{6,38},{7,39},{8,40},{9,... | collective-permute-start | bytes 3440648 | tf_op jit(solution)/shard_map/ppermute | solution.py:43
  35.3 2.5 %collective-permute-start.11 = (bf16[64,7296]{1,0:T(8,128)(2,1)S(1)}, bf16[64,7296]{1,0:T(8,128)(2,1)S(1)}, u32[]{:S(2)}, u32[]{:S(2)}) collective-permute-start(bf16[64,7296]{1,0:T(8,128)(2,1)S(1)} %collective-permute-done.7.refs_9_.refs_15_.refs_10_), channel_id=1, source_target_pairs={{0,16},{1,17},{2,18},{3,19},{4,20},{5,21},{6,22},{7,23},{8,24},{9,... | collective-permute-start | bytes 2801672 | tf_op jit(solution)/shard_map/ppermute | solution.py:43
  38.7 4.9 %collective-permute-done.10.refs_10_.refs_16_.refs_11_ = bf16[64,7296]{1,0:T(8,128)(2,1)} collective-permute-done((bf16[64,7296]{1,0:T(8,128)(2,1)S(1)}, bf16[64,7296]{1,0:T(8,128)(2,1)}, u32[]{:S(2)}, u32[]{:S(2)}) %collective-permute-start.10) | collective-permute-done | bytes 933920 | tf_op jit(solution)/shard_map/ppermute | solution.py:43
  43.6 2.8 %collective-permute-start.6 = (bf16[80,7168]{1,0:T(8,128)(2,1)}, bf16[80,7168]{1,0:T(8,128)(2,1)}, u32[]{:S(2)}, u32[]{:S(2)}) collective-permute-start(bf16[80,7168]{1,0:T(8,128)(2,1)} %collective-permute-done.2.refs_3_.refs_7_.refs_4_), channel_id=1, source_target_pairs={{0,32},{1,33},{2,34},{3,35},{4,36},{5,37},{6,38},{7,39},{8,40},{9,... | collective-permute-start | bytes 3440648 | tf_op jit(solution)/shard_map/ppermute | solution.py:43
  59.2 7.7 %shard_map.102 = (f32[640,384]{1,0:T(8,128)S(1)}, f32[3,384]{1,0:T(4,128)S(1)}) custom-call(bf16[80,7168]{1,0:T(8,128)(2,1)S(1)} %copy-done.2, bf16[80,7168]{1,0:T(8,128)(2,1)S(1)} %collective-permute-done.refs_1_.refs_5_.refs_2_, bf16[80,7168]{1,0:T(8,128)(2,1)} %collective-permute-done.1.refs_2_.refs_6_.refs_3_, ...), custom_call_target="tpu_custom_call" | custom-call | flops 3523215360 | bytes 14680064 | tf_op jit(solution)/shard_map/pallas_call | solution.py:202
  67.9 5.1 %shard_map.103 = (f32[640,128]{1,0:T(8,128)S(1)}, f32[3,128]{1,0:T(4,128)S(1)}) custom-call(bf16[80,7168]{1,0:T(8,128)(2,1)S(1)} %copy-done.2, bf16[80,7168]{1,0:T(8,128)(2,1)S(1)} %collective-permute-done.refs_1_.refs_5_.refs_2_, bf16[80,7168]{1,0:T(8,128)(2,1)} %collective-permute-done.1.refs_2_.refs_6_.refs_3_, ...), custom_call_target="tpu_custom_call" | custom-call | flops 1174405120 | bytes 11010048 | tf_op jit(solution)/shard_map/pallas_call | solution.py:202
  80.7 2.7 %collective-permute-start.19 = (f32[2,2,4,64]{3,2,1,0:T(4,128)S(1)}, f32[2,2,4,64]{3,2,1,0:T(4,128)S(1)}, u32[]{:S(2)}, u32[]{:S(2)}) collective-permute-start(f32[2,2,4,64]{3,2,1,0:T(4,128)S(1)} %get-tuple-element.79), channel_id=1, source_target_pairs={{0,80},{1,81},{2,82},{3,83},{4,84},{5,85},{6,86},{7,87},{8,88},{9,... | collective-permute-start | bytes 12296 | tf_op jit(solution)/shard_map/ppermute | solution.py:43
  84.2 3.2 %collective-permute-done.18 = f32[2,2,4,64]{3,2,1,0:T(4,128)S(1)} collective-permute-done((f32[2,2,4,64]{3,2,1,0:T(4,128)S(1)}, f32[2,2,4,64]{3,2,1,0:T(4,128)S(1)}, u32[]{:S(2)}, u32[]{:S(2)}) %collective-permute-start.18) | collective-permute-done | bytes 4128 | tf_op jit(solution)/shard_map/ppermute | solution.py:43
  88.2 11.9 %shard_map.104 = (bf16[640,512]{1,0:T(8,128)(2,1)}, bf16[64,7168]{1,0:T(8,128)(2,1)}, bf16[64,7168]{1,0:T(8,128)(2,1)}, bf16[64,7168]{1,0:T(8,128)(2,1)}, bf16[6...) custom-call(f32[640,384]{1,0:T(8,128)} %copy-done.27, ...), custom_call_target="tpu_custom_call" | custom-call | flops 4697620480 | bytes 16515072 | tf_op jit(solution)/shard_map/pallas_call | solution.py:241
  101.5 10.0 %shard_map.105 = (f32[320,7168]{1,0:T(8,128)}, bf16[320,7168]{1,0:T(8,128)(2,1)S(1)}, f32[1,7168]{1,0:T(1,128)S(1)}) custom-call(bf16[640,512]{1,0:T(8,128)(2,1)S(1)} %copy-done.29, bf16[80,7168]{1,0:T(8,128)(2,1)S(1)} %copy-done.3, bf16[80,7168]{1,0:T(8,128)(2,1)S(1)} %copy-done.7, bf16[80,7168]{1,0:T(8,128)(2,1)} %collective-permute-done.1.refs_2_.refs_6_.refs_3_, ...), custom_call_target="tpu_custom_call" | custom-call | flops 4697620480 | bytes 16515072 | tf_op jit(solution)/shard_map/pallas_call | solution.py:266
  114.7 4.2 %collective-permute-start.25 = (bf16[320,7168]{1,0:T(8,128)(2,1)S(1)}, bf16[320,7168]{1,0:T(8,128)(2,1)S(1)}, u32[]{:S(2)}, u32[]{:S(2)}) collective-permute-start(bf16[320,7168]{1,0:T(8,128)(2,1)S(1)} %get-tuple-element.64), channel_id=1, source_target_pairs={{0,32},{1,33},{2,34},{3,35},{4,36},{5,37},{6,38},{7,39},{8,40},{9,... | collective-permute-start | bytes 13762568 | tf_op jit(solution)/shard_map/ppermute | solution.py:43
  126.1 3.2 %collective-permute-start.27 = (f32[1,7168]{1,0:T(1,128)S(1)}, f32[1,7168]{1,0:T(1,128)S(1)}, u32[]{:S(2)}, u32[]{:S(2)}) collective-permute-start(f32[1,7168]{1,0:T(1,128)S(1)} %add.320), channel_id=1, source_target_pairs={{0,8},{1,9},{2,10},{3,11},{4,12},{5,13},{6,14},{7,15},{8,0},{9,1},... | collective-permute-start | bytes 86024 | tf_op jit(solution)/shard_map/ppermute | solution.py:43
  136.9 5.7 %collective-permute-done.23.refs_2_ = bf16[64,7168]{1,0:T(8,128)(2,1)S(1)} collective-permute-done((bf16[64,7168]{1,0:T(8,128)(2,1)S(1)}, bf16[64,7168]{1,0:T(8,128)(2,1)S(1)}, u32[]{:S(2)}, u32[]{:S(2)}) %collective-permute-start.23) | collective-permute-done | bytes 917536 | tf_op jit(solution)/shard_map/ppermute | solution.py:43
  144.2 2.9 %collective-permute-start.29 = (bf16[64,7168]{1,0:T(8,128)(2,1)S(1)}, bf16[64,7168]{1,0:T(8,128)(2,1)S(1)}, u32[]{:S(2)}, u32[]{:S(2)}) collective-permute-start(bf16[64,7168]{1,0:T(8,128)(2,1)S(1)} %get-tuple-element.68), channel_id=1, source_target_pairs={{0,16},{1,17},{2,18},{3,19},{4,20},{5,21},{6,22},{7,23},{8,24},{9,... | collective-permute-start | bytes 2752520 | tf_op jit(solution)/shard_map/ppermute | solution.py:43
  148.7 8.7 %collective-permute-done.31.refs_1_ = f32[1,7168]{1,0:T(1,128)S(1)} collective-permute-done((f32[1,7168]{1,0:T(1,128)S(1)}, f32[1,7168]{1,0:T(1,128)S(1)}, u32[]{:S(2)}, u32[]{:S(2)}) %collective-permute-start.31) | collective-permute-done | bytes 28704 | tf_op jit(solution)/shard_map/ppermute | solution.py:43
  163.3 3.4 %collective-permute-start.32 = (bf16[64,7168]{1,0:T(8,128)(2,1)S(1)}, bf16[64,7168]{1,0:T(8,128)(2,1)}, u32[]{:S(2)}, u32[]{:S(2)}) collective-permute-start(bf16[64,7168]{1,0:T(8,128)(2,1)S(1)} %shard_map.110.mine_ref.refs_3_), channel_id=1, source_target_pairs={{0,64},{1,65},{2,66},{3,67},{4,68},{5,69},{6,70},{7,71},{8,72},{9,... | collective-permute-start | bytes 2752520 | tf_op jit(solution)/shard_map/ppermute | solution.py:43
  166.8 4.6 %collective-permute-done.35 = f32[1,7168]{1,0:T(1,128)S(1)} collective-permute-done((f32[1,7168]{1,0:T(1,128)S(1)}, f32[1,7168]{1,0:T(1,128)S(1)}, u32[]{:S(2)}, u32[]{:S(2)}) %collective-permute-start.35) | collective-permute-done | bytes 28704 | tf_op jit(solution)/shard_map/ppermute | solution.py:43
  171.8 15.9 %collective-permute-done.36 = f32[1,7168]{1,0:T(1,128)S(1)} collective-permute-done((f32[1,7168]{1,0:T(1,128)S(1)}, f32[1,7168]{1,0:T(1,128)S(1)}, u32[]{:S(2)}, u32[]{:S(2)}) %collective-permute-start.36) | collective-permute-done | bytes 28704 | tf_op jit(solution)/shard_map/ppermute | solution.py:43
  189.9 3.1 %shard_map.111 = (bf16[64,7168]{1,0:T(8,128)(2,1)S(1)}, bf16[128,7168]{1,0:T(8,128)(2,1)}) custom-call(s32[1]{0:T(128)} %bitcast.core_ref, bf16[64,7168]{1,0:T(8,128)(2,1)S(1)} %shard_map.110.mine_ref.refs_3_, bf16[64,7168]{1,0:T(8,128)(2,1)} %collective-permute-done.32.their_ref, bf16[128,7168]{1,0:T(8,128)(2,1)S(1)} %copy-done.5, f32[1,7168]{1,0:T(1,128)S(1)} %bitcast.50), custom_call_target="tpu_custom_call" | custom-call | bytes 3670016 | tf_op jit(solution)/shard_map/pallas_call | solution.py:294
  193.4 5.8 %fusion.2 = (bf16[80,7168]{1,0:T(8,128)(2,1)}, f32[80,7168]{1,0:T(8,128)}, f32[80,7168]{1,0:T(8,128)}) fusion(bf16[80,7168]{1,0:T(8,128)(2,1)S(1)} %copy-done.3, bf16[80,7168]{1,0:T(8,128)(2,1)} %collective-permute-done.39, bf16[80,7168]{1,0:T(8,128)(2,1)} %collective-permute-done.38, bf16[320,7168]{1,0:T(8,128)(2,1)} %copy-done.1, ...), kind=kLoop, calls=%fused_computation.5 | loop fusion | flops 13189120 | bytes 17203200 | tf_op jit(solution)/shard_map/convert_element_type | solution.py:25
  (174 shorter events, 71.2 us)
Async XLA Ops:
  0.6 18.7 %collective-permute-start = (bf16[80,7168]{1,0:T(8,128)(2,1)}, bf16[80,7168]{1,0:T(8,128)(2,1)S(1)}, u32[]{:S(2)}, u32[]{:S(2)}) collective-permute-start(bf16[80,7168]{1,0:T(8,128)(2,1)} %refs_1_.1), channel_id=1, source_target_pairs={{0,12},{1,13},{2,14},{3,15},{4,0},{5,1},{6,2},{7,3},{8,4},{9,5},{1... | collective-permute-start | bytes 3440648 | tf_op jit(solution)/shard_map/ppermute | solution.py:43
  6.8 17.6 %collective-permute-start.7 = (bf16[64,7296]{1,0:T(8,128)(2,1)S(1)}, bf16[64,7296]{1,0:T(8,128)(2,1)S(1)}, u32[]{:S(2)}, u32[]{:S(2)}) collective-permute-start(bf16[64,7296]{1,0:T(8,128)(2,1)S(1)} %shard_map.101.refs_8_.refs_14_.refs_9_), channel_id=1, source_target_pairs={{0,3},{1,0},{2,1},{3,2},{4,7},{5,4},{6,5},{7,6},{8,11},{9,8},{10,9... | collective-permute-start | bytes 2801672 | tf_op jit(solution)/shard_map/ppermute | solution.py:43
  8.2 20.5 %collective-permute-start.8 = (bf16[64,7296]{1,0:T(8,128)(2,1)S(1)}, bf16[64,7296]{1,0:T(8,128)(2,1)S(1)}, u32[]{:S(2)}, u32[]{:S(2)}) collective-permute-start(bf16[64,7296]{1,0:T(8,128)(2,1)S(1)} %shard_map.101.refs_8_.refs_14_.refs_9_), channel_id=1, source_target_pairs={{0,1},{1,2},{2,3},{3,0},{4,5},{5,6},{6,7},{7,4},{8,9},{9,10},{10,1... | collective-permute-start | bytes 2801672 | tf_op jit(solution)/shard_map/ppermute | solution.py:43
  9.7 20.0 %collective-permute-start.9 = (bf16[64,7296]{1,0:T(8,128)(2,1)S(1)}, bf16[64,7296]{1,0:T(8,128)(2,1)}, u32[]{:S(2)}, u32[]{:S(2)}) collective-permute-start(bf16[64,7296]{1,0:T(8,128)(2,1)S(1)} %shard_map.101.refs_8_.refs_14_.refs_9_), channel_id=1, source_target_pairs={{0,16},{1,17},{2,18},{3,19},{4,20},{5,21},{6,22},{7,23},{8,24},{9,... | collective-permute-start | bytes 2801672 | tf_op jit(solution)/shard_map/ppermute | solution.py:43
  12.2 26.6 %collective-permute-start.2 = (bf16[80,7168]{1,0:T(8,128)(2,1)S(1)}, bf16[80,7168]{1,0:T(8,128)(2,1)}, u32[]{:S(2)}, u32[]{:S(2)}) collective-permute-start(bf16[80,7168]{1,0:T(8,128)(2,1)S(1)} %copy-done.2), channel_id=1, source_target_pairs={{0,4},{1,5},{2,6},{3,7},{4,8},{5,9},{6,10},{7,11},{8,12},{9,13},{1... | collective-permute-start | bytes 3440648 | tf_op jit(solution)/shard_map/ppermute | solution.py:43
  19.3 27.0 %collective-permute-start.1 = (bf16[80,7168]{1,0:T(8,128)(2,1)S(1)}, bf16[80,7168]{1,0:T(8,128)(2,1)}, u32[]{:S(2)}, u32[]{:S(2)}) collective-permute-start(bf16[80,7168]{1,0:T(8,128)(2,1)S(1)} %collective-permute-done.refs_1_.refs_5_.refs_2_), channel_id=1, source_target_pairs={{0,12},{1,13},{2,14},{3,15},{4,0},{5,1},{6,2},{7,3},{8,4},{9,5},{1... | collective-permute-start | bytes 3440648 | tf_op jit(solution)/shard_map/ppermute | solution.py:43
  29.6 13.9 %collective-permute-start.10 = (bf16[64,7296]{1,0:T(8,128)(2,1)S(1)}, bf16[64,7296]{1,0:T(8,128)(2,1)}, u32[]{:S(2)}, u32[]{:S(2)}) collective-permute-start(bf16[64,7296]{1,0:T(8,128)(2,1)S(1)} %collective-permute-done.7.refs_9_.refs_15_.refs_10_), channel_id=1, source_target_pairs={{0,3},{1,0},{2,1},{3,2},{4,7},{5,4},{6,5},{7,6},{8,11},{9,8},{10,9... | collective-permute-start | bytes 2801672 | tf_op jit(solution)/shard_map/ppermute | solution.py:43
  30.9 19.9 %collective-permute-start.3 = (bf16[80,7168]{1,0:T(8,128)(2,1)S(1)}, bf16[80,7168]{1,0:T(8,128)(2,1)S(1)}, u32[]{:S(2)}, u32[]{:S(2)}) collective-permute-start(bf16[80,7168]{1,0:T(8,128)(2,1)S(1)} %copy-done.2), channel_id=1, source_target_pairs={{0,32},{1,33},{2,34},{3,35},{4,36},{5,37},{6,38},{7,39},{8,40},{9,... | collective-permute-start | bytes 3440648 | tf_op jit(solution)/shard_map/ppermute | solution.py:43
  35.3 13.0 %collective-permute-start.11 = (bf16[64,7296]{1,0:T(8,128)(2,1)S(1)}, bf16[64,7296]{1,0:T(8,128)(2,1)S(1)}, u32[]{:S(2)}, u32[]{:S(2)}) collective-permute-start(bf16[64,7296]{1,0:T(8,128)(2,1)S(1)} %collective-permute-done.7.refs_9_.refs_15_.refs_10_), channel_id=1, source_target_pairs={{0,16},{1,17},{2,18},{3,19},{4,20},{5,21},{6,22},{7,23},{8,24},{9,... | collective-permute-start | bytes 2801672 | tf_op jit(solution)/shard_map/ppermute | solution.py:43
  38.7 15.6 %collective-permute-start.4 = (bf16[80,7168]{1,0:T(8,128)(2,1)S(1)}, bf16[80,7168]{1,0:T(8,128)(2,1)}, u32[]{:S(2)}, u32[]{:S(2)}) collective-permute-start(bf16[80,7168]{1,0:T(8,128)(2,1)S(1)} %collective-permute-done.refs_1_.refs_5_.refs_2_), channel_id=1, source_target_pairs={{0,32},{1,33},{2,34},{3,35},{4,36},{5,37},{6,38},{7,39},{8,40},{9,... | collective-permute-start | bytes 3440648 | tf_op jit(solution)/shard_map/ppermute | solution.py:43
  49.2 18.7 %collective-permute-start.13 = (bf16[64,7296]{1,0:T(8,128)(2,1)}, bf16[64,7296]{1,0:T(8,128)(2,1)}, u32[]{:S(2)}, u32[]{:S(2)}) collective-permute-start(bf16[64,7296]{1,0:T(8,128)(2,1)} %collective-permute-done.9.refs_12_.refs_18_.refs_13_), channel_id=1, source_target_pairs={{0,1},{1,2},{2,3},{3,0},{4,5},{5,6},{6,7},{7,4},{8,9},{9,10},{10,1... | collective-permute-start | bytes 2801672 | tf_op jit(solution)/shard_map/ppermute | solution.py:43
  51.8 16.1 %collective-permute-start.12 = (bf16[64,7296]{1,0:T(8,128)(2,1)}, bf16[64,7296]{1,0:T(8,128)(2,1)}, u32[]{:S(2)}, u32[]{:S(2)}) collective-permute-start(bf16[64,7296]{1,0:T(8,128)(2,1)} %collective-permute-done.10.refs_10_.refs_16_.refs_11_), channel_id=1, source_target_pairs={{0,16},{1,17},{2,18},{3,19},{4,20},{5,21},{6,22},{7,23},{8,24},{9,... | collective-permute-start | bytes 2801672 | tf_op jit(solution)/shard_map/ppermute | solution.py:43
  100.2 14.0 %collective-permute-start.21 = (bf16[64,7168]{1,0:T(8,128)(2,1)}, bf16[64,7168]{1,0:T(8,128)(2,1)S(1)}, u32[]{:S(2)}, u32[]{:S(2)}) collective-permute-start(bf16[64,7168]{1,0:T(8,128)(2,1)} %get-tuple-element.55), channel_id=1, source_target_pairs={{0,3},{1,0},{2,1},{3,2},{4,7},{5,4},{6,5},{7,6},{8,11},{9,8},{10,9... | collective-permute-start | bytes 2752520 | tf_op jit(solution)/shard_map/ppermute | solution.py:43
  114.7 18.1 %collective-permute-start.25 = (bf16[320,7168]{1,0:T(8,128)(2,1)S(1)}, bf16[320,7168]{1,0:T(8,128)(2,1)S(1)}, u32[]{:S(2)}, u32[]{:S(2)}) collective-permute-start(bf16[320,7168]{1,0:T(8,128)(2,1)S(1)} %get-tuple-element.64), channel_id=1, source_target_pairs={{0,32},{1,33},{2,34},{3,35},{4,36},{5,37},{6,38},{7,39},{8,40},{9,... | collective-permute-start | bytes 13762568 | tf_op jit(solution)/shard_map/ppermute | solution.py:43
  118.9 18.0 %collective-permute-start.22 = (bf16[64,7168]{1,0:T(8,128)(2,1)}, bf16[64,7168]{1,0:T(8,128)(2,1)S(1)}, u32[]{:S(2)}, u32[]{:S(2)}) collective-permute-start(bf16[64,7168]{1,0:T(8,128)(2,1)} %get-tuple-element.59), channel_id=1, source_target_pairs={{0,16},{1,17},{2,18},{3,19},{4,20},{5,21},{6,22},{7,23},{8,24},{9,... | collective-permute-start | bytes 2752520 | tf_op jit(solution)/shard_map/ppermute | solution.py:43
  120.6 22.0 %collective-permute-start.23 = (bf16[64,7168]{1,0:T(8,128)(2,1)S(1)}, bf16[64,7168]{1,0:T(8,128)(2,1)S(1)}, u32[]{:S(2)}, u32[]{:S(2)}) collective-permute-start(bf16[64,7168]{1,0:T(8,128)(2,1)S(1)} %get-tuple-element.60), channel_id=1, source_target_pairs={{0,1},{1,2},{2,3},{3,0},{4,5},{5,6},{6,7},{7,4},{8,9},{9,10},{10,1... | collective-permute-start | bytes 2752520 | tf_op jit(solution)/shard_map/ppermute | solution.py:43
  123.1 20.0 %collective-permute-start.24 = (bf16[64,7168]{1,0:T(8,128)(2,1)S(1)}, bf16[64,7168]{1,0:T(8,128)(2,1)S(1)}, u32[]{:S(2)}, u32[]{:S(2)}) collective-permute-start(bf16[64,7168]{1,0:T(8,128)(2,1)S(1)} %get-tuple-element.62), channel_id=1, source_target_pairs={{0,3},{1,0},{2,1},{3,2},{4,7},{5,4},{6,5},{7,6},{8,11},{9,8},{10,9... | collective-permute-start | bytes 2752520 | tf_op jit(solution)/shard_map/ppermute | solution.py:43
  134.6 26.3 %collective-permute-start.37 = (bf16[80,7168]{1,0:T(8,128)(2,1)S(1)}, bf16[80,7168]{1,0:T(8,128)(2,1)S(1)}, u32[]{:S(2)}, u32[]{:S(2)}) collective-permute-start(bf16[80,7168]{1,0:T(8,128)(2,1)S(1)} %get-tuple-element.73), channel_id=1, source_target_pairs={{0,4},{1,5},{2,6},{3,7},{4,8},{5,9},{6,10},{7,11},{8,12},{9,13},{1... | collective-permute-start | bytes 3440648 | tf_op jit(solution)/shard_map/ppermute | solution.py:43
  144.2 14.1 %collective-permute-start.29 = (bf16[64,7168]{1,0:T(8,128)(2,1)S(1)}, bf16[64,7168]{1,0:T(8,128)(2,1)S(1)}, u32[]{:S(2)}, u32[]{:S(2)}) collective-permute-start(bf16[64,7168]{1,0:T(8,128)(2,1)S(1)} %get-tuple-element.68), channel_id=1, source_target_pairs={{0,16},{1,17},{2,18},{3,19},{4,20},{5,21},{6,22},{7,23},{8,24},{9,... | collective-permute-start | bytes 2752520 | tf_op jit(solution)/shard_map/ppermute | solution.py:43
  147.1 13.0 %collective-permute-start.30 = (bf16[64,7168]{1,0:T(8,128)(2,1)S(1)}, bf16[64,7168]{1,0:T(8,128)(2,1)S(1)}, u32[]{:S(2)}, u32[]{:S(2)}) collective-permute-start(bf16[64,7168]{1,0:T(8,128)(2,1)S(1)} %get-tuple-element.69), channel_id=1, source_target_pairs={{0,1},{1,2},{2,3},{3,0},{4,5},{5,6},{6,7},{7,4},{8,9},{9,10},{10,1... | collective-permute-start | bytes 2752520 | tf_op jit(solution)/shard_map/ppermute | solution.py:43
  157.5 35.9 %collective-permute-start.39 = (bf16[80,7168]{1,0:T(8,128)(2,1)}, bf16[80,7168]{1,0:T(8,128)(2,1)}, u32[]{:S(2)}, u32[]{:S(2)}) collective-permute-start(bf16[80,7168]{1,0:T(8,128)(2,1)} %get-tuple-element.74), channel_id=1, source_target_pairs={{0,12},{1,13},{2,14},{3,15},{4,0},{5,1},{6,2},{7,3},{8,4},{9,5},{1... | collective-permute-start | bytes 3440648 | tf_op jit(solution)/shard_map/ppermute | solution.py:43
  161.7 31.7 %collective-permute-start.38 = (bf16[80,7168]{1,0:T(8,128)(2,1)S(1)}, bf16[80,7168]{1,0:T(8,128)(2,1)}, u32[]{:S(2)}, u32[]{:S(2)}) collective-permute-start(bf16[80,7168]{1,0:T(8,128)(2,1)S(1)} %shard_map.112), channel_id=1, source_target_pairs={{0,4},{1,5},{2,6},{3,7},{4,8},{5,9},{6,10},{7,11},{8,12},{9,13},{1... | collective-permute-start | bytes 3440648 | tf_op jit(solution)/shard_map/ppermute | solution.py:43
  163.3 25.1 %collective-permute-start.32 = (bf16[64,7168]{1,0:T(8,128)(2,1)S(1)}, bf16[64,7168]{1,0:T(8,128)(2,1)}, u32[]{:S(2)}, u32[]{:S(2)}) collective-permute-start(bf16[64,7168]{1,0:T(8,128)(2,1)S(1)} %shard_map.110.mine_ref.refs_3_), channel_id=1, source_target_pairs={{0,64},{1,65},{2,66},{3,67},{4,68},{5,69},{6,70},{7,71},{8,72},{9,... | collective-permute-start | bytes 2752520 | tf_op jit(solution)/shard_map/ppermute | solution.py:43
  171.5 16.2 %collective-permute-start.36 = (f32[1,7168]{1,0:T(1,128)S(1)}, f32[1,7168]{1,0:T(1,128)S(1)}, u32[]{:S(2)}, u32[]{:S(2)}) collective-permute-start(f32[1,7168]{1,0:T(1,128)S(1)} %add.324), channel_id=1, source_target_pairs={{0,64},{1,65},{2,66},{3,67},{4,68},{5,69},{6,70},{7,71},{8,72},{9,... | collective-permute-start | bytes 86024 | tf_op jit(solution)/shard_map/ppermute | solution.py:43
  (49 other events, 383.0 us)
